TPU v7x, 512 devices: a whole 4x8x8 slice. The times are simulated.
512 devices in a mesh: ctx: 128 (over z, y, core), head: 4 (over x).
Axes of the slice: x: 4, y: 8, z: 8, core: 2. Of those that a mesh axis runs over, the one named last changes fastest.
Arguments:
- tokens: bfloat16 [32768, 1024], P('ctx', 'head'), may hold values from -6 to 6
- q_weight: bfloat16 [1024, 1024], P(None, 'head'), may hold values from -0.1875 to 0.1875
- k_weight: bfloat16 [1024, 1024], P(None, 'head'), may hold values from -0.1875 to 0.1875
- v_weight: bfloat16 [1024, 2048], P(None, 'head'), may hold values from -0.1875 to 0.1875
- z_weight: bfloat16 [1024, 2048], P(None, 'head'), may hold values from -0.1875 to 0.1875
- a_weight: bfloat16 [1024, 16], P(None, 'head'), may hold values from -0.1875 to 0.1875
- b_weight: bfloat16 [1024, 16], P(None, 'head'), may hold values from -0.1875 to 0.1875
- conv_q: float32 [4, 1024], P(None, 'head'), may hold values from -3 to 3
- conv_k: float32 [4, 1024], P(None, 'head'), may hold values from -3 to 3
- conv_v: float32 [4, 2048], P(None, 'head'), may hold values from -3 to 3
- decay_rate: float32 [16], P('head'), may hold values from 0.5 to 16
- dt_bias: float32 [16], P('head'), may hold values from -9 to -3
- norm_gain: float32 [128], replicated, may hold values from 0.1 to 1.9
- out_weight: bfloat16 [2048, 1024], P('head'), may hold values from -0.125 to 0.125
- doc_lengths: int32 [64], replicated, may hold values from 1 to 1024, 32768 in all
Outputs:
- mixed: bfloat16 [32768, 1024], P('ctx', 'head')
Inputs may be any that keep to these rules, and one draw needn't show every extreme that they name: `doc_lengths`: 64 document lengths summing to 32768; the longest is exactly 1024.
All inputs are finite; a program needn't handle non-finite values.
Results may differ from a plain program's by a relative error of at most 0.015.
Values may be sent and summed in bfloat16 or wider, within the bound.
A program may use at most 192 MiB of HBM per device.

v0:
```python
import jax
import jax.numpy as jnp
from jax import lax
from jax.sharding import PartitionSpec as P

HV = 16
HK = 8
DK = 128
DV = 128
CH = 64
TOK_DEV = 256


highest = lax.Precision.HIGHEST


def shifted(value, axis, steps):
    count = lax.axis_size(axis)
    leading, last = (max(0, -steps), min(count, count - steps))
    return lax.ppermute(value, axis, [(source, source + steps) for source in range(leading, last)])


def segment_of(doc_lengths, positions):
    starts = jnp.cumsum(doc_lengths) - doc_lengths
    hits = (starts[None, :] <= positions[:, None]).astype(jnp.int32)
    return jnp.sum(hits, axis=1) - 1


def short_conv(inputs, before, segment, segment_before, kernel):
    kernel_len = kernel.shape[0]
    tok_rows = inputs.shape[0]
    padded = jnp.concatenate([before, inputs], axis=0).astype(jnp.float32)
    padded_seg = jnp.concatenate([segment_before, segment])
    summed = jnp.zeros(inputs.shape, jnp.float32)
    for tap_index in range(kernel_len):
        same_doc = (padded_seg[tap_index : tap_index + tok_rows] == segment)[:, None]
        summed = summed + jnp.where(
            same_doc, padded[tap_index : tap_index + tok_rows] * kernel[tap_index], 0.0
        )
    return jax.nn.silu(summed)


def unit_rows(matrix):
    return matrix / jnp.sqrt(jnp.sum(matrix * matrix, axis=-1, keepdims=True) + 1e-06)


def lower_inverse(system):
    block_len = system.shape[-1]
    identity_blk = jnp.eye(block_len, dtype=jnp.float32)
    power = -system
    result = identity_blk + power
    span = 2
    while span < block_len:
        power = jnp.einsum("...ij,...jk->...ik", power, power, precision=highest)
        result = result + jnp.einsum("...ij,...jk->...ik", result, power, precision=highest)
        span = span * 2
    return result


def block_terms(queries, keys, values, gate_log, write_rate, segment, segment_prior):
    block_len = gate_log.shape[-1]
    key_size = keys.shape[-1]
    cumulative = jnp.cumsum(gate_log, axis=-1)
    row_ids = lax.broadcasted_iota(jnp.int32, (block_len, block_len), 0)
    col_ids = lax.broadcasted_iota(jnp.int32, (block_len, block_len), 1)
    same_doc = segment[..., :, None] == segment[..., None, :]
    lower_mask = same_doc & (row_ids >= col_ids)
    strict = same_doc & (row_ids > col_ids)
    gap_log = cumulative[..., :, None] - cumulative[..., None, :]
    decays = jnp.exp(jnp.where(lower_mask, gap_log, -1e30))
    strict_decay = jnp.where(strict, decays, 0.0)
    carried = jnp.where(segment == segment_prior[..., None], jnp.exp(cumulative), 0.0)
    key_dots = jnp.einsum("...id,...jd->...ij", keys, keys, precision=highest)
    system = write_rate[..., :, None] * strict_decay * key_dots
    inverse = lower_inverse(system)
    wy_keys = jnp.einsum(
        "...ij,...jd->...id", inverse, (write_rate * carried)[..., None] * keys, precision=highest
    )
    wy_values = jnp.einsum(
        "...ij,...jd->...id", inverse, write_rate[..., None] * values, precision=highest
    )
    scores = jnp.einsum("...id,...jd->...ij", queries, keys, precision=highest) * decays
    keys_last = keys * decays[..., block_len - 1, :][..., None]
    identity_mat = jnp.eye(key_size, dtype=jnp.float32)
    transition = carried[..., block_len - 1][..., None, None] * identity_mat - jnp.einsum(
        "...jd,...je->...de", keys_last, wy_keys, precision=highest
    )
    offset = jnp.einsum("...jd,...je->...de", keys_last, wy_values, precision=highest)
    reader = queries * carried[..., None] - jnp.einsum(
        "...ij,...jd->...id", scores, wy_keys, precision=highest
    )
    local_out = jnp.einsum("...ij,...jd->...id", scores, wy_values, precision=highest)
    return (reader, local_out, transition, offset)


def gated_norm(attended, z_in, norm_gain):
    gate_vals = z_in.astype(jnp.float32).reshape(attended.shape)
    root_mean = jnp.sqrt(jnp.mean(attended * attended, axis=-1, keepdims=True) + 1e-06)
    return attended / root_mean * norm_gain * jax.nn.silu(gate_vals)


def head_matmul(left_mat, right_mat):
    return jnp.einsum("hij,hjk->hik", left_mat, right_mat, precision=highest)


def body(
    tokens,
    q_weight,
    k_weight,
    v_weight,
    z_weight,
    a_weight,
    b_weight,
    conv_q,
    conv_k,
    conv_v,
    decay_rate,
    dt_bias,
    norm_gain,
    out_weight,
    doc_lengths,
):
    tok_rows = tokens.shape[0]
    kernel_len = conv_q.shape[0]
    first_pos = lax.axis_index("ctx") * tok_rows
    positions = first_pos + jnp.arange(tok_rows, dtype=jnp.int32)
    segment = segment_of(doc_lengths, positions)
    segment_before = segment_of(
        doc_lengths, first_pos - (kernel_len - 1) + jnp.arange(kernel_len - 1, dtype=jnp.int32)
    )
    weights = (q_weight, k_weight, v_weight, z_weight, a_weight, b_weight)
    feature_cols = lax.all_gather(tokens, "head", axis=1, tiled=True)
    projected = tuple(
        (jnp.dot(feature_cols, matrix, preferred_element_type=jnp.float32) for matrix in weights)
    )
    q_in, k_in, v_in, z_in = (projection.astype(jnp.bfloat16) for projection in projected[:4])
    a_proj = projected[4]
    b_proj = projected[5]
    cut_at = tok_rows - (kernel_len - 1)
    q_tail, k_tail, v_tail = shifted((q_in[cut_at:], k_in[cut_at:], v_in[cut_at:]), "ctx", 1)
    queries = short_conv(q_in, q_tail, segment, segment_before, conv_q)
    keys = short_conv(k_in, k_tail, segment, segment_before, conv_k)
    values = short_conv(v_in, v_tail, segment, segment_before, conv_v)
    key_heads = q_in.shape[1] // DK
    value_heads = v_in.shape[1] // DV
    group_size = HV // HK
    queries = jnp.repeat(
        unit_rows(queries.reshape(tok_rows, key_heads, DK)) * DK ** (-0.5), group_size, axis=1
    )
    keys = jnp.repeat(unit_rows(keys.reshape(tok_rows, key_heads, DK)), group_size, axis=1)
    values = values.reshape(tok_rows, value_heads, DV)
    gate_log = -decay_rate * jax.nn.softplus(a_proj + dt_bias)
    write_rate = jax.nn.sigmoid(b_proj)
    block_count = tok_rows // CH

    def by_head(matrix):
        return matrix.reshape(block_count, CH, value_heads, matrix.shape[-1]).transpose(2, 0, 1, 3)

    def by_head_flat(matrix):
        return matrix.reshape(block_count, CH, value_heads).transpose(2, 0, 1)

    segment_blocks = segment.reshape(block_count, CH)
    segment_prior = jnp.concatenate([segment_before[-1:], segment_blocks[:-1, -1]])
    terms = block_terms(
        by_head(queries),
        by_head(keys),
        by_head(values),
        by_head_flat(gate_log),
        by_head_flat(write_rate),
        segment_blocks,
        segment_prior,
    )
    reader, local_out, transition, offset = tuple((jnp.moveaxis(member, 1, 0) for member in terms))
    identity_mat = jnp.broadcast_to(jnp.eye(DK, dtype=jnp.float32), (value_heads, DK, DK))
    zero_state = jnp.zeros((value_heads, DK, DV), jnp.float32)

    def compose(carry_pair, members):
        whole_mat, whole_vec = carry_pair
        block_trans, block_offset = members
        return (
            (
                head_matmul(block_trans, whole_mat),
                head_matmul(block_trans, whole_vec) + block_offset,
            ),
            None,
        )

    (whole_mat, whole_vec), _ = lax.scan(compose, (identity_mat, zero_state), (transition, offset))
    reach_shards = -(-4 * TOK_DEV // tok_rows)
    hop_count = min(lax.axis_size("ctx") - 1, reach_shards)

    def relay(hop_index, arriving):
        return shifted(head_matmul(whole_mat, arriving) + whole_vec, "ctx", 1)

    incoming = lax.fori_loop(0, hop_count, relay, zero_state)

    def advance(carry_state, members):
        block_reader, block_local, block_trans, block_offset = members
        emitted = head_matmul(block_reader, carry_state) + block_local
        return (head_matmul(block_trans, carry_state) + block_offset, emitted)

    _, block_outs = lax.scan(advance, incoming, (reader, local_out, transition, offset))
    attended = block_outs.transpose(0, 2, 1, 3).reshape(tok_rows, value_heads, DV)
    gated = (
        gated_norm(attended, z_in, norm_gain)
        .astype(jnp.bfloat16)
        .reshape(tok_rows, value_heads * DV)
    )
    head_part = jnp.dot(gated, out_weight, preferred_element_type=jnp.float32)
    return lax.psum_scatter(head_part, "head", scatter_dimension=1, tiled=True).astype(jnp.bfloat16)


def solution(mesh):
    return jax.shard_map(
        body,
        mesh=mesh,
        in_specs=(
            P("ctx", "head"),
            P(None, "head"),
            P(None, "head"),
            P(None, "head"),
            P(None, "head"),
            P(None, "head"),
            P(None, "head"),
            P(None, "head"),
            P(None, "head"),
            P(None, "head"),
            P("head"),
            P("head"),
            P(),
            P("head", None),
            P(),
        ),
        out_specs=P("ctx", "head"),
        check_vma=False,
    )
```

profile of v0, /device:TPU:16, one launch (start us, length us, event | category | flops | bytes accessed | tf_op | source)
XLA Modules:
  0.0 187.5 jit_solution(8847922996297418642)
XLA Ops:
  6.5 13.5 %all_gather.3 = bf16[256,1024]{1,0:T(8,128)(2,1)S(1)} all-gather(bf16[256,256]{1,0:T(8,128)(2,1)} %param.21), channel_id=1, replica_groups=mesh['ctx'=128,'head'=4] {'head'}, dimensions={1}, use_global_device_ids=true | all-gather | bytes 655360 | tf_op jit(solution)/shard_map/all_gather | solution.py:132
  20.3 1.9 %collective-permute-start.1 = (bf16[3,256]{1,0:T(4,128)(2,1)S(1)}, bf16[3,256]{1,0:T(4,128)(2,1)S(1)}, u32[]{:S(2)}, u32[]{:S(2)}) collective-permute-start(bf16[3,256]{1,0:T(4,128)(2,1)S(1)} %slice.143), channel_id=1, source_target_pairs={{0,4},{4,8},{8,12},{12,16},{16,20},{20,24},{24,28},{28,32},{32,36}... | collective-permute-start | bytes 4616 | tf_op jit(solution)/shard_map/ppermute | solution.py:20
  22.6 3.6 %collective-permute-start.3 = (bf16[3,256]{1,0:T(4,128)(2,1)S(1)}, bf16[3,256]{1,0:T(4,128)(2,1)S(1)}, u32[]{:S(2)}, u32[]{:S(2)}) collective-permute-start(bf16[3,256]{1,0:T(4,128)(2,1)S(1)} %slice.154), channel_id=1, source_target_pairs={{0,4},{4,8},{8,12},{12,16},{16,20},{20,24},{24,28},{28,32},{32,36}... | collective-permute-start | bytes 4616 | tf_op jit(solution)/shard_map/ppermute | solution.py:20
  28.0 1.9 %collective-permute-start.2 = (bf16[3,512]{1,0:T(4,128)(2,1)}, bf16[3,512]{1,0:T(4,128)(2,1)}, u32[]{:S(2)}, u32[]{:S(2)}) collective-permute-start(bf16[3,512]{1,0:T(4,128)(2,1)} %slice.149), channel_id=1, source_target_pairs={{0,4},{4,8},{8,12},{12,16},{16,20},{20,24},{24,28},{28,32},{32,36}... | collective-permute-start | bytes 9224 | tf_op jit(solution)/shard_map/ppermute | solution.py:20
  43.3 1.1 divide_multiply_fusion.2
  46.1 1.0 fusion.20
  51.7 1.5 fusion.73
  53.2 1.5 convolution_add_fusion.5
  55.6 1.0 convolution_multiply_fusion
  58.9 2.2 %fusion.19 = f32[4,4,128,128]{3,2,0,1:T(8,128)S(1)} fusion(f32[4,4,64,128]{3,2,1,0:T(8,128)S(1)} %fusion.38, f32[128,128]{1,0:T(8,128)S(1)} %fusion.62, f32[4,4]{0,1:T(4,128)S(1)} %bitcast.185, f32[4,4,64,128]{3,2,1,0:T(8,128)S(1)} %bitcast.171, f32[4,4,64]{2,1,0:T(4,128)S(1)} %bitcast.181), kind=kOutput, calls=%fused_computation.25 | convolution fusion | flops 201981952 | bytes 2166848 | tf_op jit(solution)/shard_map/...jd,...je->...de/dot_general | solution.py:85
  61.1 1.5 fusion.21
  65.0 1.2 divide_multiply_fusion
  66.2 2.0 %reshape_reshape.10 = f32[4,64,4,128]{3,2,1,0:T(4,128)} reshape(f32[256,512]{1,0:T(8,128)} %divide_multiply_fusion) | data formatting | bytes 1048576 | tf_op jit(solution)/shard_map/reshape;reshape | solution.py:157
  68.3 1.9 %fusion.35 = f32[4,4,64,128]{3,2,1,0:T(8,128)S(1)} fusion(f32[4,4,64,64]{3,2,1,0:T(8,128)} %copy-done.1, f32[4,64,4,128]{3,2,1,0:T(4,128)} %reshape_reshape.10, f32[4,4,64]{2,1,0:T(4,128)S(1)} %bitcast.180), kind=kOutput, calls=%fused_computation.62 | convolution fusion | flops 100794368 | bytes 1314816 | tf_op jit(solution)/shard_map/...ij,...jd->...id/dot_general | solution.py:79
  70.2 1.4 convolution_bitcast_fusion.2
  71.7 2.0 %convolution_bitcast_fusion = f32[4,4,128,128]{3,2,0,1:T(8,128)S(1)} fusion(f32[4,4,64,128]{3,2,1,0:T(8,128)S(1)} %fusion.35, f32[4,4,64,128]{3,2,1,0:T(8,128)S(1)} %bitcast.172, f32[4,4,64]{2,1,0:T(4,128)S(1)} %bitcast.182), kind=kOutput, calls=%fused_computation.23 | convolution fusion | flops 201457664 | bytes 2101248 | tf_op jit(solution)/shard_map/...jd,...je->...de/dot_general | solution.py:88
  73.7 1.1 copy.80
  74.8 7.3 %while.37 = (s32[]{:T(128)}, f32[4,128,128]{2,1,0:T(8,128)S(1)}, f32[4,128,128]{2,1,0:T(8,128)S(1)}, f32[4,4,128,128]{3,2,1,0:T(8,128)S(1)}, f32[4,4,128,128]{3,2,1,0:T(8,128)}, /*index=5*/s32[]{:T(128)}, s32[]{:T(128)}) while((s32[]{:T(128)}, f32[4,128,128]{2,1,0:T(8,128)S(1)}, f32[4,128,128]{2,1,0:T(8,128)S(1)}, ...), condition=%wide.region_6.7_spmd.clone, body=%wide.region_5.6_spmd.clone.sunk | while | flops 201457664 | bytes 2884699 | solution.py:188
  74.8 1.3 convolution_add_fusion.15
  76.6 1.3 convolution_add_fusion.15
  78.5 1.3 convolution_add_fusion.15
  80.3 1.3 convolution_add_fusion.15
  82.1 36.0 %while.35 = (s32[]{:T(128)}, f32[4,128,128]{2,1,0:T(8,128)S(1)}, f32[4,128,128]{2,1,0:T(8,128)S(1)}, f32[4,128,128]{2,1,0:T(8,128)S(1)}, s32[]{:T(128)}) while((s32[]{:T(128)}, f32[4,128,128]{2,1,0:T(8,128)S(1)}, f32[4,128,128]{2,1,0:T(8,128)S(1)}, f32[4,128,128]{2,1,0:T(8,128)S(1)}, s32[]{:T(128)}) %tuple.78), condition=%wide.region_8.9_spmd, body=%wide.region_7.8_spmd.sunk | while | flops 100728832 | bytes 2097253 | solution.py:195
  82.1 1.1 convolution_add_fusion.13
  83.2 4.8 %collective-permute-start = (f32[4,128,128]{2,1,0:T(8,128)}, f32[4,128,128]{2,1,0:T(8,128)S(1)}, u32[]{:S(2)}, u32[]{:S(2)}) collective-permute-start(f32[4,128,128]{2,1,0:T(8,128)} %convolution_add_fusion.13), channel_id=1, source_target_pairs={{0,4},{4,8},{8,12},{12,16},{16,20},{20,24},{24,28},{28,32},{32,36}... | collective-permute-start | bytes 786440 | tf_op jit(solution)/shard_map/while/body/eval_jaxpr/ppermute | solution.py:20
  88.0 3.1 %collective-permute-done = f32[4,128,128]{2,1,0:T(8,128)S(1)} collective-permute-done((f32[4,128,128]{2,1,0:T(8,128)}, f32[4,128,128]{2,1,0:T(8,128)S(1)}, u32[]{:S(2)}, u32[]{:S(2)}) %collective-permute-start) | collective-permute-done | bytes 262176 | tf_op jit(solution)/shard_map/while/body/eval_jaxpr/ppermute | solution.py:20
  91.1 1.1 convolution_add_fusion.13
  92.2 2.4 %collective-permute-start = (f32[4,128,128]{2,1,0:T(8,128)}, f32[4,128,128]{2,1,0:T(8,128)S(1)}, u32[]{:S(2)}, u32[]{:S(2)}) collective-permute-start(f32[4,128,128]{2,1,0:T(8,128)} %convolution_add_fusion.13), channel_id=1, source_target_pairs={{0,4},{4,8},{8,12},{12,16},{16,20},{20,24},{24,28},{28,32},{32,36}... | collective-permute-start | bytes 786440 | tf_op jit(solution)/shard_map/while/body/eval_jaxpr/ppermute | solution.py:20
  94.7 5.5 %collective-permute-done = f32[4,128,128]{2,1,0:T(8,128)S(1)} collective-permute-done((f32[4,128,128]{2,1,0:T(8,128)}, f32[4,128,128]{2,1,0:T(8,128)S(1)}, u32[]{:S(2)}, u32[]{:S(2)}) %collective-permute-start) | collective-permute-done | bytes 262176 | tf_op jit(solution)/shard_map/while/body/eval_jaxpr/ppermute | solution.py:20
  100.1 1.1 convolution_add_fusion.13
  101.2 2.4 %collective-permute-start = (f32[4,128,128]{2,1,0:T(8,128)}, f32[4,128,128]{2,1,0:T(8,128)S(1)}, u32[]{:S(2)}, u32[]{:S(2)}) collective-permute-start(f32[4,128,128]{2,1,0:T(8,128)} %convolution_add_fusion.13), channel_id=1, source_target_pairs={{0,4},{4,8},{8,12},{12,16},{16,20},{20,24},{24,28},{28,32},{32,36}... | collective-permute-start | bytes 786440 | tf_op jit(solution)/shard_map/while/body/eval_jaxpr/ppermute | solution.py:20
  103.7 5.5 %collective-permute-done = f32[4,128,128]{2,1,0:T(8,128)S(1)} collective-permute-done((f32[4,128,128]{2,1,0:T(8,128)}, f32[4,128,128]{2,1,0:T(8,128)S(1)}, u32[]{:S(2)}, u32[]{:S(2)}) %collective-permute-start) | collective-permute-done | bytes 262176 | tf_op jit(solution)/shard_map/while/body/eval_jaxpr/ppermute | solution.py:20
  109.1 1.1 convolution_add_fusion.13
  110.2 2.4 %collective-permute-start = (f32[4,128,128]{2,1,0:T(8,128)}, f32[4,128,128]{2,1,0:T(8,128)S(1)}, u32[]{:S(2)}, u32[]{:S(2)}) collective-permute-start(f32[4,128,128]{2,1,0:T(8,128)} %convolution_add_fusion.13), channel_id=1, source_target_pairs={{0,4},{4,8},{8,12},{12,16},{16,20},{20,24},{24,28},{28,32},{32,36}... | collective-permute-start | bytes 786440 | tf_op jit(solution)/shard_map/while/body/eval_jaxpr/ppermute | solution.py:20
  112.7 5.5 %collective-permute-done = f32[4,128,128]{2,1,0:T(8,128)S(1)} collective-permute-done((f32[4,128,128]{2,1,0:T(8,128)}, f32[4,128,128]{2,1,0:T(8,128)S(1)}, u32[]{:S(2)}, u32[]{:S(2)}) %collective-permute-start) | collective-permute-done | bytes 262176 | tf_op jit(solution)/shard_map/while/body/eval_jaxpr/ppermute | solution.py:20
  118.1 13.5 %while.36 = (s32[]{:T(128)}, f32[4,128,128]{2,1,0:T(8,128)S(1)}, f32[4,4,64,128]{3,2,1,0:T(8,128)}, f32[4,4,128,128]{3,2,1,0:T(8,128)S(1)}, f32[4,4,128,128]{3,2...) while((s32[]{:T(128)}, f32[4,128,128]{2,1,0:T(8,128)S(1)}, ...), condition=%wide.region_11.12_spmd, body=%wide.region_10.11_spmd.sunk | while | flops 151093248 | bytes 2230357 | solution.py:202
  118.1 2.0 %fusion.141 = f32[4,4,64,128]{3,2,1,0:T(8,128)} fusion(f32[4,4,64,128]{3,2,1,0:T(8,128)} %get-tuple-element.386, s32[]{:T(128)} %get-tuple-element.384, f32[4,128,128]{2,1,0:T(8,128)S(1)} %copy.135, f32[4,4,64,128]{3,2,0,1:T(8,128)} %get-tuple-element.398, f32[4,4,64,128]{3,2,0,1:T(8,128)} %get-tuple-element.397), kind=kOutput, calls=%fused_computation.4.clone.1 | convolution fusion | flops 50364416 | bytes 656384 | tf_op jit(solution)/shard_map/while/body/eval_jaxpr/hij,hjk->hik/dot_general | solution.py:103
  120.1 1.3 convolution_add_fusion.14
  121.5 2.0 %fusion.141 = f32[4,4,64,128]{3,2,1,0:T(8,128)} fusion(f32[4,4,64,128]{3,2,1,0:T(8,128)} %get-tuple-element.386, s32[]{:T(128)} %get-tuple-element.384, f32[4,128,128]{2,1,0:T(8,128)S(1)} %copy.135, f32[4,4,64,128]{3,2,0,1:T(8,128)} %get-tuple-element.398, f32[4,4,64,128]{3,2,0,1:T(8,128)} %get-tuple-element.397), kind=kOutput, calls=%fused_computation.4.clone.1 | convolution fusion | flops 50364416 | bytes 656384 | tf_op jit(solution)/shard_map/while/body/eval_jaxpr/hij,hjk->hik/dot_general | solution.py:103
  123.5 1.3 convolution_add_fusion.14
  124.9 2.0 %fusion.141 = f32[4,4,64,128]{3,2,1,0:T(8,128)} fusion(f32[4,4,64,128]{3,2,1,0:T(8,128)} %get-tuple-element.386, s32[]{:T(128)} %get-tuple-element.384, f32[4,128,128]{2,1,0:T(8,128)S(1)} %copy.135, f32[4,4,64,128]{3,2,0,1:T(8,128)} %get-tuple-element.398, f32[4,4,64,128]{3,2,0,1:T(8,128)} %get-tuple-element.397), kind=kOutput, calls=%fused_computation.4.clone.1 | convolution fusion | flops 50364416 | bytes 656384 | tf_op jit(solution)/shard_map/while/body/eval_jaxpr/hij,hjk->hik/dot_general | solution.py:103
  126.9 1.3 convolution_add_fusion.14
  128.3 2.0 %fusion.141 = f32[4,4,64,128]{3,2,1,0:T(8,128)} fusion(f32[4,4,64,128]{3,2,1,0:T(8,128)} %get-tuple-element.386, s32[]{:T(128)} %get-tuple-element.384, f32[4,128,128]{2,1,0:T(8,128)S(1)} %copy.135, f32[4,4,64,128]{3,2,0,1:T(8,128)} %get-tuple-element.398, f32[4,4,64,128]{3,2,0,1:T(8,128)} %get-tuple-element.397), kind=kOutput, calls=%fused_computation.4.clone.1 | convolution fusion | flops 50364416 | bytes 656384 | tf_op jit(solution)/shard_map/while/body/eval_jaxpr/hij,hjk->hik/dot_general | solution.py:103
  130.3 1.3 convolution_add_fusion.14
  131.6 1.3 multiply_reduce_fusion
  134.5 3.1 %fusion.37 = f32[256,1024]{1,0:T(8,128)} fusion(bf16[512,1024]{1,0:T(8,128)(2,1)S(1)} %copy-done, f32[32,8,4,128]{3,2,1,0:T(4,128)S(1)} %bitcast.176, f32[32,8,4,128]{3,2,1,0:T(4,128)S(1)} %bitcast.178, bf16[256,1024]{1,0:T(8,128)(2,1)S(1)} %all_gather.3, bf16[1024,512]{1,0:T(8,128)(2,1)} %param.25, f32[512]{0:T(512)S(1)} %copy-done.33), kind=kOutput, calls=%fused_computation.64 | convolution fusion | flops 538181632 | bytes 4720640 | tf_op jit(solution)/shard_map/dot_general | solution.py:209
  137.6 41.5 %reduce-scatter.2.cloned.1.call-done = f32[256,256]{1,0:T(8,128)} async-done(((f32[256,1024]{1,0:T(8,128)}), f32[256,256]{1,0:T(8,128)}) %reduce-scatter.2.cloned.1.call-update) | async-done | bytes 262160 | tf_op jit(solution)/shard_map/reduce_scatter | solution.py:210
  179.1 1.6 convert_element_type.67
  (173 shorter events, 30.7 us)
Async XLA Ops:
  6.5 127.3 %copy-start = (bf16[512,1024]{1,0:T(8,128)(2,1)S(1)}, bf16[512,1024]{1,0:T(8,128)(2,1)}, u32[]{:S(2)}) copy-start(bf16[512,1024]{1,0:T(8,128)(2,1)} %param.34) | copy-start | bytes 3145732
  6.5 13.5 %copy-start.11 = (bf16[1024,256]{1,0:T(8,128)(2,1)S(1)}, bf16[1024,256]{1,0:T(8,128)(2,1)}, u32[]{:S(2)}) copy-start(bf16[1024,256]{1,0:T(8,128)(2,1)} %param.23) | copy-start | bytes 1572868
  6.5 172.5 %reduce-scatter.2.cloned.1.call-start = ((), (), s32[]{:S(2)}) async-start(), calls=%async_computation.1 | async-start | bytes 1310720 | tf_op jit(solution)/shard_map/reduce_scatter | solution.py:210
  6.5 15.7 %copy-start.12 = (bf16[1024,256]{1,0:T(8,128)(2,1)S(1)}, bf16[1024,256]{1,0:T(8,128)(2,1)}, u32[]{:S(2)}) copy-start(bf16[1024,256]{1,0:T(8,128)(2,1)} %param.22) | copy-start | bytes 1572868
  20.0 6.2 %copy-start.9 = (bf16[1024,512]{1,0:T(8,128)(2,1)S(1)}, bf16[1024,512]{1,0:T(8,128)(2,1)}, u32[]{:S(2)}) copy-start(bf16[1024,512]{1,0:T(8,128)(2,1)} %param.24) | copy-start | bytes 3145732
  20.3 22.9 %collective-permute-start.1 = (bf16[3,256]{1,0:T(4,128)(2,1)S(1)}, bf16[3,256]{1,0:T(4,128)(2,1)S(1)}, u32[]{:S(2)}, u32[]{:S(2)}) collective-permute-start(bf16[3,256]{1,0:T(4,128)(2,1)S(1)} %slice.143), channel_id=1, source_target_pairs={{0,4},{4,8},{8,12},{12,16},{16,20},{20,24},{24,28},{28,32},{32,36}... | collective-permute-start | bytes 4616 | tf_op jit(solution)/shard_map/ppermute | solution.py:20
  22.6 20.6 %collective-permute-start.3 = (bf16[3,256]{1,0:T(4,128)(2,1)S(1)}, bf16[3,256]{1,0:T(4,128)(2,1)S(1)}, u32[]{:S(2)}, u32[]{:S(2)}) collective-permute-start(bf16[3,256]{1,0:T(4,128)(2,1)S(1)} %slice.154), channel_id=1, source_target_pairs={{0,4},{4,8},{8,12},{12,16},{16,20},{20,24},{24,28},{28,32},{32,36}... | collective-permute-start | bytes 4616 | tf_op jit(solution)/shard_map/ppermute | solution.py:20
  26.7 0.7 copy-start.7
  28.0 34.7 %collective-permute-start.2 = (bf16[3,512]{1,0:T(4,128)(2,1)}, bf16[3,512]{1,0:T(4,128)(2,1)}, u32[]{:S(2)}, u32[]{:S(2)}) collective-permute-start(bf16[3,512]{1,0:T(4,128)(2,1)} %slice.149), channel_id=1, source_target_pairs={{0,4},{4,8},{8,12},{12,16},{16,20},{20,24},{24,28},{28,32},{32,36}... | collective-permute-start | bytes 9224 | tf_op jit(solution)/shard_map/ppermute | solution.py:20
  29.9 0.7 copy-start.34
  32.0 0.7 copy-start.31
  32.7 10.6 %copy-start.25 = (pred[256]{0:T(512)(128)(4,1)}, pred[256]{0:T(512)(128)(4,1)S(1)}, u32[]{:S(2)}) copy-start(pred[256]{0:T(512)(128)(4,1)S(1)} %get-tuple-element.232) | copy-start | bytes 772
  32.7 10.6 %copy-start.27 = (pred[256]{0:T(512)(128)(4,1)}, pred[256]{0:T(512)(128)(4,1)S(1)}, u32[]{:S(2)}) copy-start(pred[256]{0:T(512)(128)(4,1)S(1)} %get-tuple-element.233) | copy-start | bytes 772
  32.7 10.6 %copy-start.29 = (pred[256]{0:T(512)(128)(4,1)}, pred[256]{0:T(512)(128)(4,1)S(1)}, u32[]{:S(2)}) copy-start(pred[256]{0:T(512)(128)(4,1)S(1)} %get-tuple-element.234) | copy-start | bytes 772
  32.7 0.7 copy-start.32
  32.7 1.3 copy-start.36
  33.4 0.7 copy-start.37
  34.0 0.7 copy-start.38
  34.9 0.7 copy-start.18
  35.9 0.7 copy-start.20
  38.1 0.7 copy-start.35
  41.9 0.7 copy-start.15
  45.4 0.8 copy-start.13
  53.2 1.5 copy-start.10
  55.6 1.0 copy-start.4
  55.6 1.2 copy-start.5
  56.8 4.3 %copy-start.2 = (f32[4,4,64,64]{3,2,1,0:T(8,128)}, f32[4,4,64,64]{3,2,1,0:T(8,128)S(1)}, u32[]{:S(2)}) copy-start(f32[4,4,64,64]{3,2,1,0:T(8,128)S(1)} %convolution_multiply_fusion) | copy-start | bytes 786436
  56.8 0.7 copy-start.17
  57.4 0.8 copy-start.1
  57.5 0.8 copy-start.14
  58.2 0.7 copy-start.19
  58.9 2.2 %copy-start.16 = (f32[4,4,64]{2,1,0:T(4,128)S(1)}, f32[4,4,64]{2,1,0:T(4,128)}, u32[]{:S(2)}) copy-start(f32[4,4,64]{2,1,0:T(4,128)} %copy-done.15) | copy-start | bytes 12292
  62.6 0.9 copy-start.8
  63.6 0.8 copy-start.23
  63.6 0.8 copy-start.24
  64.3 0.7 copy-start.22
  64.3 0.7 copy-start.21
  64.4 0.7 copy-start.26
  64.4 0.7 copy-start.28
  64.4 0.7 copy-start.30
  68.3 2.0 %copy-start.3 = (f32[4,4,64,64]{3,2,1,0:T(8,128)S(1)}, f32[4,4,64,64]{3,2,1,0:T(8,128)}, u32[]{:S(2)}) copy-start(f32[4,4,64,64]{3,2,1,0:T(8,128)} %copy-done.2) | copy-start | bytes 786436
  83.2 7.9 %collective-permute-start = (f32[4,128,128]{2,1,0:T(8,128)}, f32[4,128,128]{2,1,0:T(8,128)S(1)}, u32[]{:S(2)}, u32[]{:S(2)}) collective-permute-start(f32[4,128,128]{2,1,0:T(8,128)} %convolution_add_fusion.13), channel_id=1, source_target_pairs={{0,4},{4,8},{8,12},{12,16},{16,20},{20,24},{24,28},{28,32},{32,36}... | collective-permute-start | bytes 786440 | tf_op jit(solution)/shard_map/while/body/eval_jaxpr/ppermute | solution.py:20
  92.2 7.9 %collective-permute-start = (f32[4,128,128]{2,1,0:T(8,128)}, f32[4,128,128]{2,1,0:T(8,128)S(1)}, u32[]{:S(2)}, u32[]{:S(2)}) collective-permute-start(f32[4,128,128]{2,1,0:T(8,128)} %convolution_add_fusion.13), channel_id=1, source_target_pairs={{0,4},{4,8},{8,12},{12,16},{16,20},{20,24},{24,28},{28,32},{32,36}... | collective-permute-start | bytes 786440 | tf_op jit(solution)/shard_map/while/body/eval_jaxpr/ppermute | solution.py:20
  101.2 7.9 %collective-permute-start = (f32[4,128,128]{2,1,0:T(8,128)}, f32[4,128,128]{2,1,0:T(8,128)S(1)}, u32[]{:S(2)}, u32[]{:S(2)}) collective-permute-start(f32[4,128,128]{2,1,0:T(8,128)} %convolution_add_fusion.13), channel_id=1, source_target_pairs={{0,4},{4,8},{8,12},{12,16},{16,20},{20,24},{24,28},{28,32},{32,36}... | collective-permute-start | bytes 786440 | tf_op jit(solution)/shard_map/while/body/eval_jaxpr/ppermute | solution.py:20
  110.2 7.9 %collective-permute-start = (f32[4,128,128]{2,1,0:T(8,128)}, f32[4,128,128]{2,1,0:T(8,128)S(1)}, u32[]{:S(2)}, u32[]{:S(2)}) collective-permute-start(f32[4,128,128]{2,1,0:T(8,128)} %convolution_add_fusion.13), channel_id=1, source_target_pairs={{0,4},{4,8},{8,12},{12,16},{16,20},{20,24},{24,28},{28,32},{32,36}... | collective-permute-start | bytes 786440 | tf_op jit(solution)/shard_map/while/body/eval_jaxpr/ppermute | solution.py:20
  131.6 1.5 copy-start.6
  133.8 0.7 copy-start.33
Sparse Core Ops, SparseCore 0:
  137.7 41.2 reduce-scatter.1
where the time goes:
time: 189 us; the launch traced here: 188 us
  waiting for transfers between devices  60.9 us (32%)
  matrix products  49.2 us (26%)
  starting transfers between devices  19.5 us (10%)
  local copies, waits for them, and re-layouts  18.5 us (10%)
  between operations  14.1 us (7%)
  blocking collectives  13.5 us (7%)
  other arithmetic  11.5 us (6%)
    reduce_scatter x1, waiting for transfers between devices, body(): lax.psum_scatter(head_part, 'head', scatter_dimension=1, tiled=True)  41.5 us
    dot_general x20, matrix products, head_matmul(): return jnp.einsum('hij,hjk->hik', left_mat, right_mat, precision=highest)  24.7 us
    ppermute x7, starting transfers between devices, shifted(): lax.ppermute(value, axis, [(source, source + steps) for source in range(l...  19.5 us
    ppermute x7, waiting for transfers between devices, shifted(): lax.ppermute(value, axis, [(source, source + steps) for source in range(l...  19.5 us
    all_gather x1, blocking collectives, body(): feature_cols = lax.all_gather(tokens, 'head', axis=1, tiled=True)  13.5 us
    unnamed x80, local copies, waits for them, and re-layouts  10.8 us
    dot_general x5, matrix products, lower_inverse(): jnp.einsum('...ij,...jk->...ik', result, power, precision=highest)  4.05 us
    dot_general x5, matrix products, lower_inverse(): power = jnp.einsum('...ij,...jk->...ik', power, power, precision=highest)  4.03 us
  transfers between devices with their start and end apart: 8, of which 5 were waited for; matrix products, arithmetic and copies ran while one was open for 14% of the time, Pallas kernels for 0%

commit v1 on v0

v1 whole, which is shorter than its diff:
```python
import jax
import jax.numpy as jnp
from jax import lax
from jax.experimental import pallas as pl
from jax.experimental.pallas import tpu as pltpu
from jax.sharding import PartitionSpec as P

DK = 128
HALO = 16
MESH = pl.DeviceIdType.MESH
f32 = jnp.float32
bf16 = jnp.bfloat16


def dot(left, right):
    return jnp.dot(left, right, preferred_element_type=f32)


def dot_t(left, right):
    return lax.dot_general(left, right, (((1,), (1,)), ((), ())), preferred_element_type=f32)


def silu(u):
    return u / (1.0 + jnp.exp(-u))


def iotas(rows, cols):
    return (
        lax.broadcasted_iota(jnp.int32, (rows, cols), 0),
        lax.broadcasted_iota(jnp.int32, (rows, cols), 1),
    )


def layer_kernel(
    n_ctx,
    n_head,
    doc,
    rate,
    dtb,
    tok,
    wq_h,
    wk_h,
    wv_h,
    wz_h,
    wa_h,
    wb_h,
    cq_h,
    ck_h,
    cv_h,
    gain_h,
    wo_h,
    out,
    xg,
    wall,
    wz,
    wa,
    wb,
    wo,
    conv,
    gain,
    acc,
    zbuf,
    eq,
    mm,
    taps,
    neg,
    cmask,
    kvb,
    abuf,
    pbuf,
    wub,
    to_s,
    to_r,
    och_s,
    och_r,
    se_s,
    sin_r,
    tchip,
    ochip,
    s_use,
    obuf,
    rbuf,
    osum,
    load_sem,
    halo_send,
    halo_recv,
    ag_send,
    ag_recv,
    to_send,
    to_recv,
    och_send,
    och_recv,
    se_send,
    sin_recv,
    rs_send,
    rs_recv,
):
    rows = tok.shape[0]
    feat = tok.shape[1]
    heads = 4
    i = lax.axis_index("ctx")
    j = lax.axis_index("head")
    core = lax.rem(i, 2)

    def ctx_at(step):
        return lax.rem(i + step + n_ctx, n_ctx)

    def head_at(step):
        return lax.rem(j + step + n_head, n_head)

    right, left, diag = head_at(1), head_at(-1), head_at(2)

    loads = [
        (tok, xg.at[j, pl.ds(HALO, rows), :]),
        (wk_h, wall.at[:, pl.ds(256, 256)]),
        (wv_h, wall.at[:, pl.ds(512, 512)]),
        (wq_h, wall.at[:, pl.ds(0, 256)]),
        (wa_h, wa),
        (wb_h, wb),
        (cq_h, conv.at[:, pl.ds(0, 256)]),
        (ck_h, conv.at[:, pl.ds(256, 256)]),
        (cv_h, conv.at[:, pl.ds(512, 512)]),
        (wz_h, wz),
        (wo_h, wo),
        (gain_h, gain),
    ]
    loads = [
        pltpu.make_async_copy(src, dst, load_sem.at[n]) for n, (src, dst) in enumerate(loads)
    ]
    for copy in loads:
        copy.start()

    barrier = pltpu.get_barrier_semaphore()
    peers = [(i, head_at(d)) for d in (1, 2, 3)]
    peers += [(ctx_at(-1), head_at(d)) for d in range(4)]
    peers += [(ctx_at(-2), j)]
    for peer in peers:
        pl.semaphore_signal(barrier, inc=1, device_id=peer, device_id_type=MESH)
    pl.semaphore_wait(barrier, len(peers))

    def remote(src, dst, send, recv, to):
        return pltpu.make_async_remote_copy(
            src_ref=src, dst_ref=dst, send_sem=send, recv_sem=recv, device_id=to, device_id_type=MESH
        )

    half = rows // 2
    lo, hi = pl.ds(HALO, half), pl.ds(HALO + half, half)
    tok_lo, tok_hi = tok.at[pl.ds(0, half), :], tok.at[pl.ds(half, half), :]
    halo = [
        remote(
            tok.at[pl.ds(rows - HALO, HALO), :],
            xg.at[j, pl.ds(0, HALO), :],
            halo_send.at[d],
            halo_recv.at[d],
            (ctx_at(1), head_at(d)),
        )
        for d in range(4)
    ]
    ring = [
        remote(tok_lo, xg.at[j, lo, :], ag_send.at[0], ag_recv.at[0], (i, right)),
        remote(tok_hi, xg.at[j, hi, :], ag_send.at[1], ag_recv.at[1], (i, right)),
        remote(tok_hi, xg.at[j, hi, :], ag_send.at[2], ag_recv.at[2], (i, left)),
        remote(tok_lo, xg.at[j, lo, :], ag_send.at[3], ag_recv.at[3], (i, left)),
        remote(xg.at[left, lo, :], xg.at[left, lo, :], ag_send.at[4], ag_recv.at[4], (i, right)),
        remote(xg.at[right, hi, :], xg.at[right, hi, :], ag_send.at[5], ag_recv.at[5], (i, left)),
    ]
    for copy in halo:
        copy.start()
    ring[0].start()
    ring[2].start()
    ring[1].start()
    ring[3].start()

    row_id, col_id = iotas(256, 256)

    def same(size):
        return (row_id // size == col_id // size).astype(f32)

    levels = [same(size) for size in (8, 16, 32, 64, 128)] + [jnp.ones((256, 256), f32)]
    mm[0] = jnp.where(row_id > col_id, levels[0], 0.0).astype(bf16)
    for n in range(5):
        mm[n + 1] = (levels[n + 1] - levels[n]).astype(bf16)
    for n in range(4):
        eq[n] = levels[n + 1].astype(bf16)
    eq[4] = (row_id >= col_id).astype(bf16)

    first = i * rows
    pos = first + lax.broadcasted_iota(jnp.int32, (8, 256), 1)

    def doc_step(n, carry):
        start, found = carry
        found = jnp.where(pos >= start, start, found)
        return start + doc[n], found

    _, found = lax.fori_loop(0, doc.shape[0], doc_step, (jnp.int32(0), jnp.zeros((8, 256), jnp.int32)))
    start_row = (found - first).astype(f32)
    start_col = jnp.broadcast_to(start_row[0:1, :], (128, 256)).T
    row_f = lax.broadcasted_iota(jnp.int32, (256, 128), 0).astype(f32)
    col_f = lax.broadcasted_iota(jnp.int32, (256, 128), 1).astype(f32)
    for n in range(3):
        taps[n] = jnp.where(row_f - (3 - n) >= start_col, 1.0, 0.0)
    for n in range(2):
        col_n = col_f + 128.0 * n
        neg[:, 128 * n : 128 * n + 128] = jnp.where(
            (col_n <= row_f) & (col_n >= start_col), 0.0, -1e30
        )
    cmask[...] = jnp.where(start_col < 0.0, 1.0, 0.0)

    lane = lax.broadcasted_iota(jnp.int32, (1, 128), 1)
    rate_row = jnp.zeros((1, 128), f32)
    dt_row = jnp.zeros((1, 128), f32)
    for h in range(heads):
        rate_row = jnp.where(lane == h, rate[h], rate_row)
        dt_row = jnp.where(lane == h, dtb[h], dt_row)

    for copy in loads[:6]:
        copy.wait()
    wall[:, 1024:1152] = jnp.concatenate(
        [wa[...], wb[...], jnp.zeros((wa.shape[0], 120), bf16)], axis=1
    )

    def slice_dot(slot):
        weights = wall[pl.ds(pl.multiple_of(slot * feat, feat), feat), :]
        return dot(xg[slot], weights)

    for copy in halo:
        copy.wait_recv()
    acc[...] = slice_dot(j)
    ring[0].wait_recv()
    ring[4].start()
    ring[2].wait_recv()
    ring[5].start()
    ring[1].wait_recv()
    acc[...] += slice_dot(left)
    ring[3].wait_recv()
    acc[...] += slice_dot(right)
    ring[4].wait_recv()
    ring[5].wait_recv()
    acc[...] += slice_dot(diag)
    acc[:, 0:1024] = acc[:, 0:1024].astype(bf16).astype(f32)

    ab = acc[HALO:, 1024:1152]
    pre = ab + dt_row
    gate = -rate_row * (jnp.maximum(pre, 0.0) + jnp.log1p(jnp.exp(-jnp.abs(pre))))
    beta = 1.0 / (1.0 + jnp.exp(-ab))
    g1 = gate.astype(bf16)
    g2 = (gate - g1.astype(f32)).astype(bf16)
    g3 = (gate - g1.astype(f32) - g2.astype(f32)).astype(bf16)
    tri = eq[4]
    cum = dot(tri, g1) + dot(tri, g2) + dot(tri, g3)
    cum_row = cum.T
    carried = jnp.exp(cum) * cmask[...]

    for copy in loads[6:9]:
        copy.wait()

    def short_conv(col):
        cols = slice(col, col + 128)
        total = acc[HALO:, cols] * conv[3:4, cols]
        for n in range(3):
            total += acc[HALO - 3 + n : HALO - 3 + n + rows, cols] * conv[n : n + 1, cols] * taps[n]
        return silu(total)

    def unit(matrix):
        return matrix * lax.rsqrt(jnp.sum(matrix * matrix, axis=-1, keepdims=True) + 1e-06)

    k_unit = [unit(short_conv(256 + 128 * n)) for n in range(2)]
    k_bf = [k.astype(bf16) for k in k_unit]
    k_dots = [dot_t(k, k) for k in k_bf]
    k_trans = [k.T for k in k_unit]
    q_unit = [unit(short_conv(128 * n)) * (DK**-0.5) for n in range(2)]
    q_dots = [dot_t(q_unit[n].astype(bf16), k_bf[n]) for n in range(2)]

    last_rows = []
    for h in range(heads):
        kh = h // 2
        decay = jnp.exp(cum[:, h : h + 1] - cum_row[h : h + 1, :] + neg[...])
        b_col = beta[:, 4 + h : 5 + h]
        abuf[h] = (k_dots[kh] * decay * b_col).astype(bf16)
        pbuf[h] = (q_dots[kh] * decay).astype(bf16)
        last_rows.append(decay[rows - 1 : rows, :])
        kvb[h, :, 0:128] = (k_unit[kh] * (b_col * carried[:, h : h + 1])).astype(bf16)
        kvb[h, :, 128:256] = (short_conv(512 + 128 * h) * b_col).astype(bf16)

    def expand(compact, level):
        size = compact.shape[0]
        return jnp.concatenate([compact.astype(bf16)] * (256 // size), axis=0) * eq[level]

    row16, col16 = iotas(16, 256)
    eye16 = (row16 == col16 % 16).astype(f32)
    every = range(heads)
    a8 = [abuf[h] * mm[0] for h in every]
    a8c = [sum(a8[h][16 * n : 16 * n + 16, :].astype(f32) for n in range(16)) for h in every]
    p2 = [dot(a8c[h].astype(bf16), a8[h]) for h in every]
    p2f = [expand(p2[h], 0) for h in every]
    x1 = [eye16 - a8c[h] for h in every]
    x2 = [x1[h] + dot(x1[h].astype(bf16), p2f[h]) for h in every]
    p4 = [dot(p2[h].astype(bf16), p2f[h]) for h in every]
    p4f = [expand(p4[h], 0) for h in every]
    d = [x2[h] + dot(x2[h].astype(bf16), p4f[h]) for h in every]
    y = [dot(d[h].astype(bf16), abuf[h] * mm[1]) for h in every]
    d = [d[h] - dot(y[h].astype(bf16), expand(d[h], 0)) for h in every]
    for n, size in enumerate((16, 32, 64, 128)):
        odd = (lax.broadcasted_iota(jnp.int32, (1, 256), 1) // size) % 2 == 1
        y = [dot(d[h].astype(bf16), abuf[h] * mm[n + 2]) for h in every]
        z = [dot(y[h].astype(bf16), expand(d[h], n)) for h in every]
        d = [
            jnp.concatenate([jnp.where(odd, 0.0, d[h]), jnp.where(odd, d[h], 0.0) - z[h]], axis=0)
            for h in every
        ]
    for h in every:
        wub[h] = dot(d[h].astype(bf16), kvb[h]).astype(bf16)

    row_k, col_k = iotas(128, 128)
    for h in every:
        k_last = (k_trans[h // 2] * last_rows[h]).astype(bf16)
        step = dot(k_last, wub[h])
        passed = jnp.where(row_k == col_k, carried[rows - 1 : rows, h : h + 1], 0.0)
        to_s[h, :, 0:128] = (passed - step[:, 0:128]).astype(bf16)
        to_s[h, :, 128:256] = step[:, 128:256].astype(bf16)

    to_copy = [
        remote(to_s.at[h], to_r.at[h], to_send.at[h], to_recv.at[h], (ctx_at(1), j)) for h in every
    ]
    och_copy = [
        remote(och_s.at[h], och_r.at[h], och_send.at[h], och_recv.at[h], (ctx_at(2), j))
        for h in every
    ]
    se_copy = [
        [
            remote(se_s.at[h], sin_r.at[h], se_send.at[n, h], sin_recv.at[h], (ctx_at(n + 1), j))
            for n in range(2)
        ]
        for h in every
    ]

    @pl.when(core == 0)
    def _():
        for copy in to_copy:
            copy.start()

    reader, local = [], []
    for h in every:
        seen = dot(pbuf[h], wub[h])
        reader.append((q_unit[h // 2] * carried[:, h : h + 1] - seen[:, 0:128]).astype(bf16))
        local.append(seen[:, 128:256])

    @pl.when(core == 1)
    def _():
        for h in every:
            to_copy[h].wait_recv()
            both = dot(to_s[h, :, 0:128], to_r[h])
            tchip[h] = both[:, 0:128].astype(bf16)
            total = both[:, 128:256] + to_s[h, :, 128:256].astype(f32)
            ochip[h] = total
            och_s[h] = total.astype(bf16)
            och_copy[h].start()

    loads[9].wait()
    z_in = jnp.zeros((rows, 512), f32)
    for n in range(4):
        z_in += dot(xg[n, HALO:, :], wz[feat * n : feat * n + feat, :])
    loads[11].wait()
    gain_row = gain[...].reshape(1, 128)
    z_in = silu(z_in.astype(bf16).astype(f32))
    for h in every:
        zbuf[:, 128 * h : 128 * h + 128] = z_in[:, 128 * h : 128 * h + 128] * gain_row

    @pl.when(core == 1)
    def _():
        for h in every:
            och_copy[h].wait_recv()
            se_s[h] = (dot(tchip[h], och_r[h]) + ochip[h]).astype(bf16)
            for copy in se_copy[h]:
                copy.start()

    loads[10].wait()

    for h in every:
        se_copy[h][0].wait_recv()

    @pl.when(core == 0)
    def _():
        s_use[...] = sin_r[...]

    @pl.when(core == 1)
    def _():
        for h in every:
            s_use[h] = (
                dot(to_r[h, :, 0:128], sin_r[h]) + to_r[h, :, 128:256].astype(f32)
            ).astype(bf16)

    gated = []
    for h in every:
        attended = dot(reader[h], s_use[h]) + local[h]
        scale = lax.rsqrt(jnp.mean(attended * attended, axis=-1, keepdims=True) + 1e-06)
        gated.append((attended * scale * zbuf[:, 128 * h : 128 * h + 128]).astype(bf16))
    gated = jnp.concatenate(gated, axis=1)

    def part(slot):
        return dot(gated, wo[:, pl.ds(pl.multiple_of(slot * feat, feat), feat)])

    rs_copy = []
    for n, step in enumerate((2, 1, 3)):
        slot = head_at(step)
        obuf[n] = part(slot).astype(bf16)
        copy = remote(obuf.at[n], rbuf.at[n], rs_send.at[n], rs_recv.at[n], (i, slot))
        copy.start()
        rs_copy.append(copy)
    osum[...] = part(j)
    for copy in rs_copy:
        copy.wait_recv()
    out[...] = (
        osum[...] + rbuf[0].astype(f32) + rbuf[1].astype(f32) + rbuf[2].astype(f32)
    ).astype(bf16)

    for copy in halo + ring + rs_copy:
        copy.wait_send()

    @pl.when(core == 0)
    def _():
        for copy in to_copy:
            copy.wait_send()

    @pl.when(core == 1)
    def _():
        for copy in och_copy:
            copy.wait_send()
        for pair in se_copy:
            for copy in pair:
                copy.wait_send()


def body(n_ctx, n_head, *arrays):
    (
        tokens,
        q_weight,
        k_weight,
        v_weight,
        z_weight,
        a_weight,
        b_weight,
        conv_q,
        conv_k,
        conv_v,
        decay_rate,
        dt_bias,
        norm_gain,
        out_weight,
        doc_lengths,
    ) = arrays
    rows, feat = tokens.shape
    smem = pl.BlockSpec(memory_space=pltpu.SMEM)
    hbm = pl.BlockSpec(memory_space=pl.ANY)
    vmem = pltpu.VMEM
    dma = pltpu.SemaphoreType.DMA
    return pl.pallas_call(
        lambda *refs: layer_kernel(n_ctx, n_head, *refs),
        out_shape=jax.ShapeDtypeStruct((rows, feat), bf16),
        in_specs=[smem] * 3 + [hbm] * 12,
        out_specs=pl.BlockSpec(memory_space=pltpu.VMEM),
        scratch_shapes=[
            vmem((4, HALO + rows, feat), bf16),
            vmem((1024, 1152), bf16),
            vmem((1024, 512), bf16),
            vmem((1024, 4), bf16),
            vmem((1024, 4), bf16),
            vmem((512, 1024), bf16),
            vmem((4, 1024), f32),
            vmem((128,), f32),
            vmem((HALO + rows, 1152), f32),
            vmem((rows, 512), f32),
            vmem((5, 256, 256), bf16),
            vmem((6, 256, 256), bf16),
            vmem((3, 256, 128), f32),
            vmem((256, 256), f32),
            vmem((256, 128), f32),
            vmem((4, 256, 256), bf16),
            vmem((4, 256, 256), bf16),
            vmem((4, 256, 256), bf16),
            vmem((4, 256, 256), bf16),
            vmem((4, 128, 256), bf16),
            vmem((4, 128, 256), bf16),
            vmem((4, 128, 128), bf16),
            vmem((4, 128, 128), bf16),
            vmem((4, 128, 128), bf16),
            vmem((4, 128, 128), bf16),
            vmem((4, 128, 128), bf16),
            vmem((4, 128, 128), f32),
            vmem((4, 128, 128), bf16),
            vmem((3, rows, feat), bf16),
            vmem((3, rows, feat), bf16),
            vmem((rows, feat), f32),
            dma((12,)),
            dma((4,)),
            dma((4,)),
            dma((6,)),
            dma((6,)),
            dma((4,)),
            dma((4,)),
            dma((4,)),
            dma((4,)),
            dma((2, 4)),
            dma((4,)),
            dma((3,)),
            dma((3,)),
        ],
        compiler_params=pltpu.CompilerParams(
            collective_id=0, has_side_effects=True, vmem_limit_bytes=48 * 1024 * 1024
        ),
        name="delta_layer",
    )(
        doc_lengths,
        decay_rate,
        dt_bias,
        tokens,
        q_weight,
        k_weight,
        v_weight,
        z_weight,
        a_weight,
        b_weight,
        conv_q,
        conv_k,
        conv_v,
        norm_gain,
        out_weight,
    )


def solution(mesh):
    n_ctx, n_head = mesh.shape["ctx"], mesh.shape["head"]
    return jax.shard_map(
        lambda *arrays: body(n_ctx, n_head, *arrays),
        mesh=mesh,
        in_specs=(
            P("ctx", "head"),
            P(None, "head"),
            P(None, "head"),
            P(None, "head"),
            P(None, "head"),
            P(None, "head"),
            P(None, "head"),
            P(None, "head"),
            P(None, "head"),
            P(None, "head"),
            P("head"),
            P("head"),
            P(),
            P("head", None),
            P(),
        ),
        out_specs=P("ctx", "head"),
        check_vma=False,
    )
```

time: 189 us -> 58.7 us (0.31)
  the two profiles are of different devices: /device:TPU:16 before, /device:TPU:1 now
where the time goes in v1:
time: 58.7 us; the launch traced here: 58.3 us
  Pallas kernels  47.4 us (81%)
  local copies, waits for them, and re-layouts  10.8 us (18%)
    pallas_call x1, Pallas kernels, body(): pl.pallas_call(lambda *refs: layer_kernel(n_ctx, n_head, *refs), out_shap...  47.4 us
    unnamed x29, local copies, waits for them, and re-layouts  10.8 us

profile of v1, /device:TPU:1, one launch (start us, length us, event | category | flops | bytes accessed | tf_op | source)
XLA Modules:
  0.0 58.3 jit_solution(14929901805039005177)
XLA Ops:
  0.0 0.0 copy-start.3
  0.0 1.0 %copy.16.refs_8_ = bf16[1024,4]{1,0:T(8,128)(2,1)S(1)} copy(bf16[1024,4]{0,1:T(4,128)(2,1)} %param.20) | data formatting | bytes 16384 | tf_op args[5]
  1.0 0.0 copy-start.6
  1.0 0.0 copy-start.7
  1.0 0.0 copy-start.8
  1.0 0.9 %copy.17.refs_9_ = bf16[1024,4]{1,0:T(8,128)(2,1)S(1)} copy(bf16[1024,4]{0,1:T(4,128)(2,1)} %param.21) | data formatting | bytes 16384 | tf_op args[6]
  1.9 0.0 copy-done.3
  1.9 0.0 copy-done.6
  1.9 0.0 copy-done.7
  1.9 0.0 copy-done.8
  2.0 0.0 copy-start
  2.0 1.2 %copy-done = bf16[1024,512]{1,0:T(8,128)(2,1)S(1)} copy-done((bf16[1024,512]{1,0:T(8,128)(2,1)S(1)}, bf16[1024,512]{1,0:T(8,128)(2,1)}, u32[]{:S(2)}) %copy-start) | copy-done | bytes 1048600
  3.2 0.0 copy-start.1
  3.2 1.2 %copy-done.1 = bf16[1024,512]{1,0:T(8,128)(2,1)S(1)} copy-done((bf16[1024,512]{1,0:T(8,128)(2,1)S(1)}, bf16[1024,512]{1,0:T(8,128)(2,1)}, u32[]{:S(2)}) %copy-start.1) | copy-done | bytes 1048600
  4.4 0.0 copy-start.2
  4.4 1.2 %copy-done.2 = bf16[512,1024]{1,0:T(8,128)(2,1)S(1)} copy-done((bf16[512,1024]{1,0:T(8,128)(2,1)S(1)}, bf16[512,1024]{1,0:T(8,128)(2,1)}, u32[]{:S(2)}) %copy-start.2) | copy-done | bytes 1048600
  5.6 0.0 copy-start.4
  5.6 1.0 %copy-done.4 = bf16[1024,256]{1,0:T(8,128)(2,1)S(1)} copy-done((bf16[1024,256]{1,0:T(8,128)(2,1)S(1)}, bf16[1024,256]{1,0:T(8,128)(2,1)}, u32[]{:S(2)}) %copy-start.4) | copy-done | bytes 524312
  6.7 0.0 copy-start.5
  6.7 0.9 %copy-done.5 = bf16[256,256]{1,0:T(8,128)(2,1)S(1)} copy-done((bf16[256,256]{1,0:T(8,128)(2,1)S(1)}, bf16[256,256]{1,0:T(8,128)(2,1)}, u32[]{:S(2)}) %copy-start.5) | copy-done | bytes 131096
  7.6 0.0 copy-start.9
  7.6 0.7 %copy-done.9 = s32[64]{0:T(128)S(1)} copy-done((s32[64]{0:T(128)S(1)}, s32[64]{0:T(128)}, u32[]{:S(2)}) %copy-start.9) | copy-done | bytes 280
  8.2 0.0 copy-start.10
  8.2 0.7 %copy-done.10 = f32[4]{0:T(128)S(1)} copy-done((f32[4]{0:T(128)S(1)}, f32[4]{0:T(128)}, u32[]{:S(2)}) %copy-start.10) | copy-done | bytes 40
  8.9 0.0 copy-start.11
  8.9 0.7 %copy-done.11 = f32[4]{0:T(128)S(1)} copy-done((f32[4]{0:T(128)S(1)}, f32[4]{0:T(128)}, u32[]{:S(2)}) %copy-start.11) | copy-done | bytes 40
  9.5 0.0 copy-start.12
  9.6 0.7 %copy-done.12 = f32[128]{0:T(128)S(1)} copy-done((f32[128]{0:T(128)S(1)}, f32[128]{0:T(128)}, u32[]{:S(2)}) %copy-start.12) | copy-done | bytes 536
  10.2 47.4 %delta_layer.1 = bf16[256,256]{1,0:T(8,128)(2,1)S(1)} custom-call(s32[64]{0:T(128)S(1)} %copy-done.9, f32[4]{0:T(128)S(1)} %copy-done.10, f32[4]{0:T(128)S(1)} %copy-done.11, bf16[256,256]{1,0:T(8,128)(2,1)S(1)} %copy-done.5, bf16[1024,256]{1,0:T(8,128)(2,1)S(1)} %copy-done.3, bf16[1024,256]{1,0:T(8,128)(2,1)S(1)} %copy-done.4, ...), custom_call_target="tpu_custom_call" | custom-call | tf_op jit(solution)/shard_map/delta_layer/pallas_call | solution.py:457
  57.7 0.7 %copy.19 = bf16[256,256]{1,0:T(8,128)(2,1)} copy(bf16[256,256]{1,0:T(8,128)(2,1)S(1)} %delta_layer.1) | data formatting | bytes 262144
Async XLA Ops:
  0.0 1.9 %copy-start.3 = (bf16[1024,256]{1,0:T(8,128)(2,1)S(1)}, bf16[1024,256]{1,0:T(8,128)(2,1)}, u32[]{:S(2)}) copy-start(bf16[1024,256]{1,0:T(8,128)(2,1)} %refs_4_.1) | copy-start | bytes 1572868
  1.0 1.0 %copy-start.6 = (f32[4,512]{1,0:T(4,128)S(1)}, f32[4,512]{1,0:T(4,128)}, u32[]{:S(2)}) copy-start(f32[4,512]{1,0:T(4,128)} %refs_12_.1) | copy-start | bytes 24580
  1.0 1.0 %copy-start.7 = (f32[4,256]{1,0:T(4,128)S(1)}, f32[4,256]{1,0:T(4,128)}, u32[]{:S(2)}) copy-start(f32[4,256]{1,0:T(4,128)} %refs_10_.1) | copy-start | bytes 12292
  1.0 1.0 %copy-start.8 = (f32[4,256]{1,0:T(4,128)S(1)}, f32[4,256]{1,0:T(4,128)}, u32[]{:S(2)}) copy-start(f32[4,256]{1,0:T(4,128)} %refs_11_.1) | copy-start | bytes 12292
  2.0 1.2 %copy-start = (bf16[1024,512]{1,0:T(8,128)(2,1)S(1)}, bf16[1024,512]{1,0:T(8,128)(2,1)}, u32[]{:S(2)}) copy-start(bf16[1024,512]{1,0:T(8,128)(2,1)} %refs_6_.1) | copy-start | bytes 3145732
  3.2 1.2 %copy-start.1 = (bf16[1024,512]{1,0:T(8,128)(2,1)S(1)}, bf16[1024,512]{1,0:T(8,128)(2,1)}, u32[]{:S(2)}) copy-start(bf16[1024,512]{1,0:T(8,128)(2,1)} %refs_7_.1) | copy-start | bytes 3145732
  4.4 1.2 %copy-start.2 = (bf16[512,1024]{1,0:T(8,128)(2,1)S(1)}, bf16[512,1024]{1,0:T(8,128)(2,1)}, u32[]{:S(2)}) copy-start(bf16[512,1024]{1,0:T(8,128)(2,1)} %refs_14_.1) | copy-start | bytes 3145732
  5.6 1.0 %copy-start.4 = (bf16[1024,256]{1,0:T(8,128)(2,1)S(1)}, bf16[1024,256]{1,0:T(8,128)(2,1)}, u32[]{:S(2)}) copy-start(bf16[1024,256]{1,0:T(8,128)(2,1)} %refs_5_.1) | copy-start | bytes 1572868
  6.7 0.9 %copy-start.5 = (bf16[256,256]{1,0:T(8,128)(2,1)S(1)}, bf16[256,256]{1,0:T(8,128)(2,1)}, u32[]{:S(2)}) copy-start(bf16[256,256]{1,0:T(8,128)(2,1)} %refs_3_.1) | copy-start | bytes 393220
  7.6 0.7 %copy-start.9 = (s32[64]{0:T(128)S(1)}, s32[64]{0:T(128)}, u32[]{:S(2)}) copy-start(s32[64]{0:T(128)} %refs_0_.1) | copy-start | bytes 772
  8.2 0.7 %copy-start.10 = (f32[4]{0:T(128)S(1)}, f32[4]{0:T(128)}, u32[]{:S(2)}) copy-start(f32[4]{0:T(128)} %refs_1_.1) | copy-start | bytes 52
  8.9 0.7 %copy-start.11 = (f32[4]{0:T(128)S(1)}, f32[4]{0:T(128)}, u32[]{:S(2)}) copy-start(f32[4]{0:T(128)} %refs_2_.1) | copy-start | bytes 52
  9.5 0.7 %copy-start.12 = (f32[128]{0:T(128)S(1)}, f32[128]{0:T(128)}, u32[]{:S(2)}) copy-start(f32[128]{0:T(128)} %refs_13_.1) | copy-start | bytes 1540

commit v2 on v1

v2 whole, which is shorter than its diff:
```python
import jax
import jax.numpy as jnp
from jax import lax
from jax.experimental import pallas as pl
from jax.experimental.pallas import tpu as pltpu
from jax.sharding import PartitionSpec as P

DK = 128
HALO = 16
MESH = pl.DeviceIdType.MESH
f32 = jnp.float32
bf16 = jnp.bfloat16


def dot(left, right):
    return jnp.dot(left, right, preferred_element_type=f32)


def dot_t(left, right):
    return lax.dot_general(left, right, (((1,), (1,)), ((), ())), preferred_element_type=f32)


def silu(u):
    return u / (1.0 + jnp.exp(-u))


def iotas(rows, cols):
    return (
        lax.broadcasted_iota(jnp.int32, (rows, cols), 0),
        lax.broadcasted_iota(jnp.int32, (rows, cols), 1),
    )


def layer_kernel(
    n_ctx,
    n_head,
    doc_h,
    rate_h,
    dtb_h,
    tok,
    wq_h,
    wk_h,
    wv_h,
    wz_h,
    wa_h,
    wb_h,
    cq_h,
    ck_h,
    cv_h,
    gain_h,
    wo_h,
    out,
    doc,
    rate,
    dtb,
    xg,
    wall,
    wz,
    wab,
    wo,
    conv,
    gain,
    acc,
    zbuf,
    eq,
    mm,
    taps,
    neg,
    cmask,
    kvb,
    abuf,
    wub,
    reader,
    local,
    to_s,
    pair,
    chip_s,
    chip_r,
    off_s,
    off_r,
    use_s,
    s_use,
    obuf,
    rbuf,
    osum,
    load_sem,
    halo_send,
    halo_recv,
    ag_send,
    ag_recv,
    to_send,
    to_recv,
    chip_send,
    chip_recv,
    off_send,
    off_recv,
    use_send,
    use_recv,
    rs_send,
    rs_recv,
):
    rows = tok.shape[0]
    feat = tok.shape[1]
    heads = 4
    every = range(heads)
    i = lax.axis_index("ctx")
    j = lax.axis_index("head")
    core = lax.rem(i, 2)

    def ctx_at(step):
        return lax.rem(i + step + n_ctx, n_ctx)

    def head_at(step):
        return lax.rem(j + step + n_head, n_head)

    mate = (i + 1 - 2 * core, j)

    barrier = pltpu.get_barrier_semaphore()
    peers = [(i, head_at(d)) for d in (1, 2, 3)]
    peers += [(ctx_at(-1), head_at(d)) for d in every]
    peers += [(ctx_at(1), j), (ctx_at(-2), j), (ctx_at(-4), j)]
    for peer in peers:
        pl.semaphore_signal(barrier, inc=1, device_id=peer, device_id_type=MESH)

    loads = [
        (tok, xg.at[j, pl.ds(HALO, rows), :]),
        (wk_h, wall.at[:, pl.ds(0, 256)]),
        (wv_h, wall.at[:, pl.ds(256, 512)]),
        (wq_h, wall.at[:, pl.ds(896, 256)]),
        (wa_h, wab.at[0]),
        (wb_h, wab.at[1]),
        (ck_h, conv.at[:, pl.ds(0, 256)]),
        (cv_h, conv.at[:, pl.ds(256, 512)]),
        (cq_h, conv.at[:, pl.ds(768, 256)]),
        (wz_h, wz),
        (wo_h, wo),
        (gain_h, gain),
        (doc_h, doc),
        (rate_h, rate),
        (dtb_h, dtb),
    ]
    loads = [
        pltpu.make_async_copy(src, dst, load_sem.at[n]) for n, (src, dst) in enumerate(loads)
    ]
    for copy in loads:
        copy.start()

    def remote(src, dst, send, recv, to):
        return pltpu.make_async_remote_copy(
            src_ref=src, dst_ref=dst, send_sem=send, recv_sem=recv, device_id=to, device_id_type=MESH
        )

    halo = [
        remote(
            tok.at[pl.ds(rows - HALO, HALO), :],
            xg.at[j, pl.ds(0, HALO), :],
            halo_send.at[d],
            halo_recv.at[d],
            (ctx_at(1), head_at(d)),
        )
        for d in every
    ]
    gather = {
        d: remote(
            tok,
            xg.at[j, pl.ds(HALO, rows), :],
            ag_send.at[d - 1],
            ag_recv.at[d - 1],
            (i, head_at(d)),
        )
        for d in (1, 3, 2)
    }
    pl.semaphore_wait(barrier, len(peers))
    for copy in halo:
        copy.start()
    for copy in gather.values():
        copy.start()

    row_id, col_id = iotas(256, 256)
    apart = row_id ^ col_id
    levels = [(apart < size).astype(f32) for size in (8, 16, 32, 64, 128)] + [
        jnp.ones((256, 256), f32)
    ]
    mm[0] = jnp.where(row_id > col_id, levels[0], 0.0).astype(bf16)
    for n in range(5):
        mm[n + 1] = (levels[n + 1] - levels[n]).astype(bf16)
    for n in range(4):
        eq[n] = levels[n + 1].astype(bf16)
    eq[4] = jnp.where(row_id >= col_id, 1.0, 0.0).astype(bf16)

    for copy in loads[12:]:
        copy.wait()
    first = i * rows
    pos = first + lax.broadcasted_iota(jnp.int32, (8, 256), 1)

    def doc_step(n, carry):
        start, found = carry
        found = jnp.where(pos >= start, start, found)
        return start + doc[n], found

    _, found = lax.fori_loop(
        0, doc.shape[0], doc_step, (jnp.int32(0), jnp.zeros((8, 256), jnp.int32)), unroll=8
    )
    start_row = (found - first).astype(f32)
    start_col = jnp.broadcast_to(start_row[0:1, :], (128, 256)).T
    row_f = lax.broadcasted_iota(jnp.int32, (256, 128), 0).astype(f32)
    col_f = lax.broadcasted_iota(jnp.int32, (256, 128), 1).astype(f32)
    for n in range(3):
        taps[n] = jnp.where(row_f - (3 - n) >= start_col, 1.0, 0.0)
    for n in range(2):
        col_n = col_f + 128.0 * n
        neg[:, 128 * n : 128 * n + 128] = jnp.where(
            (col_n <= row_f) & (col_n >= start_col), 0.0, -1e30
        )
    cmask[...] = jnp.where(start_col < 0.0, 1.0, 0.0)

    lane = lax.broadcasted_iota(jnp.int32, (1, 128), 1)
    rate_row = jnp.zeros((1, 128), f32)
    dt_row = jnp.zeros((1, 128), f32)
    for h in every:
        rate_row = jnp.where(lane == h, rate[h], rate_row)
        dt_row = jnp.where(lane == h, dtb[h], dt_row)

    for copy in loads[:9]:
        copy.wait()
    wab_t = jnp.concatenate(
        [wab[0].astype(f32), wab[1].astype(f32), jnp.zeros((120, wab.shape[2]), f32)], axis=0
    )
    wall[:, 768:896] = wab_t.T.astype(bf16)

    def slice_dot(slot, begin, end):
        weights = wall[pl.ds(pl.multiple_of(slot * feat, feat), feat), begin:end]
        return dot(xg[slot], weights)

    def rounded(value):
        return value.astype(bf16).astype(f32)

    for copy in halo:
        copy.wait_recv()
    acc[...] = slice_dot(j, 0, 1152)
    gather[1].wait_recv()
    acc[...] += slice_dot(head_at(-1), 0, 1152)
    gather[3].wait_recv()
    acc[...] += slice_dot(head_at(1), 0, 1152)
    gather[2].wait_recv()
    acc[:, 768:896] += slice_dot(head_at(2), 768, 896)
    acc[:, 0:256] = rounded(acc[:, 0:256] + slice_dot(head_at(2), 0, 256))
    acc[:, 256:768] = rounded(acc[:, 256:768] + slice_dot(head_at(2), 256, 768))

    ab = acc[HALO:, 768:896]
    pre = ab + dt_row
    gate = -rate_row * (jnp.maximum(pre, 0.0) + jnp.log1p(jnp.exp(-jnp.abs(pre))))
    beta = 1.0 / (1.0 + jnp.exp(-ab))
    g1 = gate.astype(bf16)
    g2 = (gate - g1.astype(f32)).astype(bf16)
    g3 = (gate - g1.astype(f32) - g2.astype(f32)).astype(bf16)
    tri = eq[4]
    cum = dot(tri, g1) + dot(tri, g2) + dot(tri, g3)
    cum_row = cum.T
    carried = jnp.exp(cum) * cmask[...]

    def short_conv(col, tap):
        cols = slice(col, col + 128)
        weights = conv[:, tap : tap + 128]
        total = acc[HALO:, cols] * weights[3:4]
        for n in range(3):
            total += acc[HALO - 3 + n : HALO - 3 + n + rows, cols] * weights[n : n + 1] * taps[n]
        return silu(total)

    def unit(matrix):
        return matrix * lax.rsqrt(jnp.sum(matrix * matrix, axis=-1, keepdims=True) + 1e-06)

    def decay_of(h):
        return jnp.exp(cum[:, h : h + 1] - cum_row[h : h + 1, :] + neg[...])

    k_unit = [unit(short_conv(128 * n, 128 * n)) for n in range(2)]
    k_bf = [k.astype(bf16) for k in k_unit]
    k_dots = [dot_t(k, k) for k in k_bf]
    k_trans = [k.T for k in k_unit]
    last_rows = []
    for h in every:
        kh = h // 2
        decay = decay_of(h)
        b_col = beta[:, 4 + h : 5 + h]
        abuf[h] = (k_dots[kh] * decay * b_col).astype(bf16)
        last_rows.append(decay[rows - 1 : rows, :])
        kvb[h, :, 0:128] = (k_unit[kh] * (b_col * carried[:, h : h + 1])).astype(bf16)
        kvb[h, :, 128:256] = (short_conv(256 + 128 * h, 256 + 128 * h) * b_col).astype(bf16)

    def expand(compact, level):
        size = compact.shape[0]
        return jnp.concatenate([compact.astype(bf16)] * (256 // size), axis=0) * eq[level]

    row16, col16 = iotas(16, 256)
    eye16 = (row16 == (col16 & 15)).astype(f32)
    a8 = [abuf[h] * mm[0] for h in every]
    a8c = [sum(a8[h][16 * n : 16 * n + 16, :].astype(f32) for n in range(16)) for h in every]
    p2 = [dot(a8c[h].astype(bf16), a8[h]) for h in every]
    p2f = [expand(p2[h], 0) for h in every]
    x1 = [eye16 - a8c[h] for h in every]
    x2 = [x1[h] + dot(x1[h].astype(bf16), p2f[h]) for h in every]
    p4 = [dot(p2[h].astype(bf16), p2f[h]) for h in every]
    p4f = [expand(p4[h], 0) for h in every]
    d = [x2[h] + dot(x2[h].astype(bf16), p4f[h]) for h in every]
    y = [dot(d[h].astype(bf16), abuf[h] * mm[1]) for h in every]
    d = [d[h] - dot(y[h].astype(bf16), expand(d[h], 0)) for h in every]
    for n, size in enumerate((16, 32, 64, 128)):
        odd = (lax.broadcasted_iota(jnp.int32, (1, 256), 1) & size) != 0
        y = [dot(d[h].astype(bf16), abuf[h] * mm[n + 2]) for h in every]
        z = [dot(y[h].astype(bf16), expand(d[h], n)) for h in every]
        d = [
            jnp.concatenate([jnp.where(odd, 0.0, d[h]), jnp.where(odd, d[h], 0.0) - z[h]], axis=0)
            for h in every
        ]
    for h in every:
        wub[h] = dot(d[h].astype(bf16), kvb[h]).astype(bf16)

    row_k, col_k = iotas(128, 128)
    for h in every:
        k_last = (k_trans[h // 2] * last_rows[h]).astype(bf16)
        step = dot(k_last, wub[h])
        passed = jnp.where(row_k == col_k, carried[rows - 1 : rows, h : h + 1], 0.0)
        to_s[h, :, 0:128] = (passed - step[:, 0:128]).astype(bf16)
        to_s[h, :, 128:256] = step[:, 128:256].astype(bf16)

    to_copy = [
        remote(to_s.at[2 - 2 * core + n], pair.at[core, n], to_send.at[n], to_recv.at[n], mate)
        for n in range(2)
    ]
    for copy in to_copy:
        copy.start()
    for n in range(2):
        pair[core, n] = to_s[2 * core + n]
    next_copy, after_copy = [], []
    for n in range(2):
        to_copy[n].wait_recv()
        both = dot(pair[1, n, :, 0:128], pair[0, n])
        chip_s[n, :, 0:128] = both[:, 0:128].astype(bf16)
        offset = (both[:, 128:256] + pair[1, n, :, 128:256].astype(f32)).astype(bf16)
        chip_s[n, :, 128:256] = offset
        off_s[n] = offset
        after_copy.append(
            remote(off_s.at[n], off_r.at[n], off_send.at[n], off_recv.at[n], (ctx_at(4), j))
        )
        next_copy.append(
            remote(chip_s.at[n], chip_r.at[n], chip_send.at[n], chip_recv.at[n], (ctx_at(2), j))
        )
        after_copy[n].start()
        next_copy[n].start()

    q_cols = slice(896, 1152)
    acc[:, q_cols] = rounded(acc[:, q_cols] + slice_dot(head_at(2), 896, 1152))
    q_unit = [unit(short_conv(896 + 128 * n, 768 + 128 * n)) * (DK**-0.5) for n in range(2)]
    q_dots = [dot_t(q_unit[n].astype(bf16), k_bf[n]) for n in range(2)]
    for h in every:
        seen = dot((q_dots[h // 2] * decay_of(h)).astype(bf16), wub[h])
        reader[h] = (q_unit[h // 2] * carried[:, h : h + 1] - seen[:, 0:128]).astype(bf16)
        local[h] = seen[:, 128:256]

    for copy in loads[9:12]:
        copy.wait()
    z_in = jnp.zeros((rows, 512), f32)
    for n in range(4):
        z_in += dot(xg[n, HALO:, :], wz[feat * n : feat * n + feat, :])
    gain_row = gain[...].reshape(1, 128)
    z_in = silu(rounded(z_in))
    for h in every:
        zbuf[:, 128 * h : 128 * h + 128] = z_in[:, 128 * h : 128 * h + 128] * gain_row

    use_copy = [
        remote(use_s.at[n], s_use.at[2 * core + n], use_send.at[n], use_recv.at[n], mate)
        for n in range(2)
    ]
    first_core = core == 0
    for n in range(2):
        after_copy[n].wait_recv()
        next_copy[n].wait_recv()
        s_in = dot(chip_r[n, :, 0:128], off_r[n]) + chip_r[n, :, 128:256].astype(f32)
        s_mid = dot(pair[0, n, :, 0:128], s_in.astype(bf16)) + pair[0, n, :, 128:256].astype(f32)
        use_s[n] = jnp.where(first_core, s_mid, s_in).astype(bf16)
        use_copy[n].start()
        s_use[2 * core + n] = jnp.where(first_core, s_in, s_mid).astype(bf16)
    for copy in use_copy:
        copy.wait_recv()

    chunk = rows // 2
    rs_copy = []
    for c in range(2):
        span = slice(chunk * c, chunk * c + chunk)
        gated = []
        for h in every:
            attended = dot(reader[h, span, :], s_use[h]) + local[h, span, :]
            scale = lax.rsqrt(jnp.mean(attended * attended, axis=-1, keepdims=True) + 1e-06)
            gated.append((attended * scale * zbuf[span, 128 * h : 128 * h + 128]).astype(bf16))
        gated = jnp.concatenate(gated, axis=1)
        for n, d_step in enumerate((2, 1, 3)):
            slot = head_at(d_step)
            weights = wo[:, pl.ds(pl.multiple_of(slot * feat, feat), feat)]
            obuf[n, span, :] = dot(gated, weights).astype(bf16)
            copy = remote(
                obuf.at[n, pl.ds(chunk * c, chunk), :],
                rbuf.at[n, pl.ds(chunk * c, chunk), :],
                rs_send.at[c, n],
                rs_recv.at[c, n],
                (i, slot),
            )
            copy.start()
            rs_copy.append(copy)
        osum[span, :] = dot(gated, wo[:, pl.ds(pl.multiple_of(j * feat, feat), feat)])
    for c in range(2):
        span = slice(chunk * c, chunk * c + chunk)
        for copy in rs_copy[3 * c : 3 * c + 3]:
            copy.wait_recv()
        total = osum[span, :]
        for n in range(3):
            total += rbuf[n, span, :].astype(f32)
        out[span, :] = total.astype(bf16)

    gathers = [gather[d] for d in (1, 3, 2)]
    for copy in halo + gathers + to_copy + next_copy + after_copy + use_copy + rs_copy:
        copy.wait_send()


def body(n_ctx, n_head, *arrays):
    (
        tokens,
        q_weight,
        k_weight,
        v_weight,
        z_weight,
        a_weight,
        b_weight,
        conv_q,
        conv_k,
        conv_v,
        decay_rate,
        dt_bias,
        norm_gain,
        out_weight,
        doc_lengths,
    ) = arrays
    rows, feat = tokens.shape
    hbm = pl.BlockSpec(memory_space=pltpu.HBM)
    vmem = pltpu.VMEM
    dma = pltpu.SemaphoreType.DMA
    return pl.pallas_call(
        lambda *refs: layer_kernel(n_ctx, n_head, *refs),
        out_shape=jax.ShapeDtypeStruct((rows, feat), bf16),
        in_specs=[hbm] * 15,
        out_specs=pl.BlockSpec(memory_space=pltpu.VMEM),
        scratch_shapes=[
            pltpu.SMEM((64,), jnp.int32),
            pltpu.SMEM((4,), f32),
            pltpu.SMEM((4,), f32),
            vmem((4, HALO + rows, feat), bf16),
            vmem((1024, 1152), bf16),
            vmem((1024, 512), bf16),
            vmem((2, 4, 1024), bf16),
            vmem((512, 1024), bf16),
            vmem((4, 1024), f32),
            vmem((128,), f32),
            vmem((HALO + rows, 1152), f32),
            vmem((rows, 512), f32),
            vmem((5, 256, 256), bf16),
            vmem((6, 256, 256), bf16),
            vmem((3, 256, 128), f32),
            vmem((256, 256), f32),
            vmem((256, 128), f32),
            vmem((4, 256, 256), bf16),
            vmem((4, 256, 256), bf16),
            vmem((4, 256, 256), bf16),
            vmem((4, 256, 128), bf16),
            vmem((4, 256, 128), f32),
            vmem((4, 128, 256), bf16),
            vmem((2, 2, 128, 256), bf16),
            vmem((2, 128, 256), bf16),
            vmem((2, 128, 256), bf16),
            vmem((2, 128, 128), bf16),
            vmem((2, 128, 128), bf16),
            vmem((2, 128, 128), bf16),
            vmem((4, 128, 128), bf16),
            vmem((3, rows, feat), bf16),
            vmem((3, rows, feat), bf16),
            vmem((rows, feat), f32),
            dma((15,)),
            dma((4,)),
            dma((4,)),
            dma((3,)),
            dma((3,)),
            dma((2,)),
            dma((2,)),
            dma((2,)),
            dma((2,)),
            dma((2,)),
            dma((2,)),
            dma((2,)),
            dma((2,)),
            dma((2, 3)),
            dma((2, 3)),
        ],
        compiler_params=pltpu.CompilerParams(
            collective_id=0, has_side_effects=True, vmem_limit_bytes=60 * 1024 * 1024
        ),
        name="delta_layer",
    )(
        doc_lengths,
        decay_rate,
        dt_bias,
        tokens,
        q_weight,
        k_weight,
        v_weight,
        z_weight,
        a_weight.T,
        b_weight.T,
        conv_q,
        conv_k,
        conv_v,
        norm_gain,
        out_weight,
    )


def solution(mesh):
    n_ctx, n_head = mesh.shape["ctx"], mesh.shape["head"]
    return jax.shard_map(
        lambda *arrays: body(n_ctx, n_head, *arrays),
        mesh=mesh,
        in_specs=(
            P("ctx", "head"),
            P(None, "head"),
            P(None, "head"),
            P(None, "head"),
            P(None, "head"),
            P(None, "head"),
            P(None, "head"),
            P(None, "head"),
            P(None, "head"),
            P(None, "head"),
            P("head"),
            P("head"),
            P(),
            P("head", None),
            P(),
        ),
        out_specs=P("ctx", "head"),
        check_vma=False,
    )
```

time: 58.7 us -> 49.1 us (0.84)
  local copies, waits for them, and re-layouts: 10.8 us -> 1.57 us
    unnamed x29 -> x1, local copies, waits for them, and re-layouts: 10.8 us -> 1.57 us
where the time goes in v2:
time: 49.1 us; the launch traced here: 49 us
  Pallas kernels  47.4 us (97%)
  local copies, waits for them, and re-layouts  1.57 us (3%)
    pallas_call x1, Pallas kernels, body(): pl.pallas_call(lambda *refs: layer_kernel(n_ctx, n_head, *refs), out_shap...  47.4 us
    unnamed x1, local copies, waits for them, and re-layouts  1.57 us

profile of v2, /device:TPU:1, one launch (start us, length us, event | category | flops | bytes accessed | tf_op | source)
XLA Modules:
  0.0 49.0 jit_solution(16825146372349613360)
XLA Ops:
  0.0 47.4 %delta_layer.1 = bf16[256,256]{1,0:T(8,128)(2,1)} custom-call(s32[64]{0:T(128)} %refs_0_.1, f32[4]{0:T(128)} %refs_1_.1, f32[4]{0:T(128)} %refs_2_.1, bf16[256,256]{1,0:T(8,128)(2,1)} %refs_3_.1, bf16[1024,256]{1,0:T(8,128)(2,1)} %refs_4_.1, bf16[1024,256]{1,0:T(8,128)(2,1)} %refs_5_.1, bf16[1024,512]{1,0:T(8,128)(2,1)} %refs_6_.1, ...), custom_call_target="tpu_custom_call" | custom-call | tf_op jit(solution)/shard_map/delta_layer/pallas_call | solution.py:446
  47.4 1.6 %copy.17 = bf16[256,256]{1,0:T(8,128)(2,1)} copy(bf16[256,256]{1,0:T(8,128)(2,1)} %delta_layer.1) | data formatting | bytes 262144

commit v3 on v2

--- a/solution.py
+++ b/solution.py
@@ -108,7 +108,10 @@
     core = lax.rem(i, 2)
 
     def ctx_at(step):
-        return lax.rem(i + step + n_ctx, n_ctx)
+        return jnp.clip(i + step, 0, n_ctx - 1)
+
+    def there(step):
+        return (i + step < n_ctx) if step > 0 else (i + step >= 0)
 
     def head_at(step):
         return lax.rem(j + step + n_head, n_head)
@@ -116,11 +119,18 @@
     mate = (i + 1 - 2 * core, j)
 
     barrier = pltpu.get_barrier_semaphore()
-    peers = [(i, head_at(d)) for d in (1, 2, 3)]
-    peers += [(ctx_at(-1), head_at(d)) for d in every]
-    peers += [(ctx_at(1), j), (ctx_at(-2), j), (ctx_at(-4), j)]
-    for peer in peers:
-        pl.semaphore_signal(barrier, inc=1, device_id=peer, device_id_type=MESH)
+    def greet(*to):
+        for one in to:
+            pl.semaphore_signal(barrier, inc=1, device_id=one, device_id_type=MESH)
+
+    greet(*[(i, head_at(d)) for d in (1, 2, 3)])
+    pl.when(there(-1))(lambda: greet(*[(ctx_at(-1), head_at(d)) for d in every]))
+    pl.when(core == 0)(lambda: greet((ctx_at(1), j)))
+    pl.when(there(-2))(lambda: greet((ctx_at(-2), j)))
+    pl.when(there(-4))(lambda: greet((ctx_at(-4), j)))
+    expected = 3 + core + sum(
+        jnp.where(there(step), number, 0) for step, number in ((1, 4), (2, 1), (4, 1))
+    )
 
     loads = [
         (tok, xg.at[j, pl.ds(HALO, rows), :]),
@@ -170,11 +180,15 @@
         )
         for d in (1, 3, 2)
     }
-    pl.semaphore_wait(barrier, len(peers))
-    for copy in halo:
-        copy.start()
+    pl.semaphore_wait(barrier, expected)
     for copy in gather.values():
         copy.start()
+
+    @pl.when(there(1))
+    def _():
+        for copy in halo:
+            copy.start()
+
 
     row_id, col_id = iotas(256, 256)
     apart = row_id ^ col_id
@@ -235,8 +249,15 @@
     def rounded(value):
         return value.astype(bf16).astype(f32)
 
-    for copy in halo:
-        copy.wait_recv()
+    @pl.when(there(-1))
+    def _():
+        for copy in halo:
+            copy.wait_recv()
+
+    @pl.when(i == 0)
+    def _():
+        xg[:, 0:HALO, :] = jnp.zeros((4, HALO, feat), bf16)
+
     acc[...] = slice_dot(j, 0, 1152)
     gather[1].wait_recv()
     acc[...] += slice_dot(head_at(-1), 0, 1152)
@@ -345,8 +366,8 @@
         next_copy.append(
             remote(chip_s.at[n], chip_r.at[n], chip_send.at[n], chip_recv.at[n], (ctx_at(2), j))
         )
-        after_copy[n].start()
-        next_copy[n].start()
+        pl.when(there(4))(after_copy[n].start)
+        pl.when(there(2))(next_copy[n].start)
 
     q_cols = slice(896, 1152)
     acc[:, q_cols] = rounded(acc[:, q_cols] + slice_dot(head_at(2), 896, 1152))
@@ -372,9 +393,18 @@
         for n in range(2)
     ]
     first_core = core == 0
+
+    @pl.when(i < 2)
+    def _():
+        chip_r[...] = jnp.zeros(chip_r.shape, bf16)
+
+    @pl.when(i < 4)
+    def _():
+        off_r[...] = jnp.zeros(off_r.shape, bf16)
+
     for n in range(2):
-        after_copy[n].wait_recv()
-        next_copy[n].wait_recv()
+        pl.when(there(-4))(after_copy[n].wait_recv)
+        pl.when(there(-2))(next_copy[n].wait_recv)
         s_in = dot(chip_r[n, :, 0:128], off_r[n]) + chip_r[n, :, 128:256].astype(f32)
         s_mid = dot(pair[0, n, :, 0:128], s_in.astype(bf16)) + pair[0, n, :, 128:256].astype(f32)
         use_s[n] = jnp.where(first_core, s_mid, s_in).astype(bf16)
@@ -417,8 +447,14 @@
         out[span, :] = total.astype(bf16)
 
     gathers = [gather[d] for d in (1, 3, 2)]
-    for copy in halo + gathers + to_copy + next_copy + after_copy + use_copy + rs_copy:
+    for copy in gathers + to_copy + use_copy + rs_copy:
         copy.wait_send()
+    for step, copies in ((1, halo), (2, next_copy), (4, after_copy)):
+
+        @pl.when(there(step))
+        def _(copies=copies):
+            for copy in copies:
+                copy.wait_send()
 
 
 def body(n_ctx, n_head, *arrays):

time: 49.1 us -> 40.6 us (0.83)
  the two profiles are of different devices: /device:TPU:1 before, /device:TPU:449 now
where the time goes in v3:
time: 40.6 us; the launch traced here: 40.4 us
  Pallas kernels  38.9 us (96%)
  local copies, waits for them, and re-layouts  1.57 us (4%)
    pallas_call x1, Pallas kernels, body(): pl.pallas_call(lambda *refs: layer_kernel(n_ctx, n_head, *refs), out_shap...  38.9 us
    unnamed x1, local copies, waits for them, and re-layouts  1.57 us

profile of v3, /device:TPU:449, one launch (start us, length us, event | category | flops | bytes accessed | tf_op | source)
XLA Modules:
  0.0 40.4 jit_solution(7691706766702098756)
XLA Ops:
  0.0 38.9 %delta_layer.1 = bf16[256,256]{1,0:T(8,128)(2,1)} custom-call(s32[64]{0:T(128)} %refs_0_.1, f32[4]{0:T(128)} %refs_1_.1, f32[4]{0:T(128)} %refs_2_.1, bf16[256,256]{1,0:T(8,128)(2,1)} %refs_3_.1, bf16[1024,256]{1,0:T(8,128)(2,1)} %refs_4_.1, bf16[1024,256]{1,0:T(8,128)(2,1)} %refs_5_.1, bf16[1024,512]{1,0:T(8,128)(2,1)} %refs_6_.1, ...), custom_call_target="tpu_custom_call" | custom-call | tf_op jit(solution)/shard_map/delta_layer/pallas_call | solution.py:482
  38.9 1.6 %copy.17 = bf16[256,256]{1,0:T(8,128)(2,1)} copy(bf16[256,256]{1,0:T(8,128)(2,1)} %delta_layer.1) | data formatting | bytes 262144

commit v4 on v3

--- a/solution.py
+++ b/solution.py
@@ -21,7 +21,7 @@
 
 
 def silu(u):
-    return u / (1.0 + jnp.exp(-u))
+    return (0.5 * u) * (1.0 + jnp.tanh(0.5 * u))
 
 
 def iotas(rows, cols):
@@ -152,9 +152,6 @@
     loads = [
         pltpu.make_async_copy(src, dst, load_sem.at[n]) for n, (src, dst) in enumerate(loads)
     ]
-    for copy in loads:
-        copy.start()
-
     def remote(src, dst, send, recv, to):
         return pltpu.make_async_remote_copy(
             src_ref=src, dst_ref=dst, send_sem=send, recv_sem=recv, device_id=to, device_id_type=MESH
@@ -170,18 +167,26 @@
         )
         for d in every
     ]
-    gather = {
-        d: remote(
-            tok,
-            xg.at[j, pl.ds(HALO, rows), :],
-            ag_send.at[d - 1],
-            ag_recv.at[d - 1],
-            (i, head_at(d)),
+    edge = rows // 4
+    right, left = head_at(1), head_at(-1)
+
+    def move(number, owner, begin, count, to):
+        source = xg.at[owner, pl.ds(HALO + begin, count), :]
+        mine = tok.at[pl.ds(begin, count), :]
+        return remote(
+            mine if owner is j else source, source, ag_send.at[number], ag_recv.at[number], (i, to)
         )
-        for d in (1, 3, 2)
-    }
+
+    gather = [
+        move(0, j, 0, edge, right),
+        move(1, j, rows - edge, edge, left),
+        move(2, j, edge, rows - 2 * edge, head_at(2)),
+        move(3, j, edge, rows - edge, right),
+        move(4, j, 0, rows - edge, left),
+    ]
+    forward = [move(5, left, 0, edge, right), move(6, right, rows - edge, edge, left)]
     pl.semaphore_wait(barrier, expected)
-    for copy in gather.values():
+    for copy in gather:
         copy.start()
 
     @pl.when(there(1))
@@ -189,6 +194,8 @@
         for copy in halo:
             copy.start()
 
+    for copy in loads:
+        copy.start()
 
     row_id, col_id = iotas(256, 256)
     apart = row_id ^ col_id
@@ -235,6 +242,10 @@
         rate_row = jnp.where(lane == h, rate[h], rate_row)
         dt_row = jnp.where(lane == h, dtb[h], dt_row)
 
+    for n in range(2):
+        gather[n].wait_recv()
+        forward[n].start()
+
     for copy in loads[:9]:
         copy.wait()
     wab_t = jnp.concatenate(
@@ -259,15 +270,32 @@
         xg[:, 0:HALO, :] = jnp.zeros((4, HALO, feat), bf16)
 
     acc[...] = slice_dot(j, 0, 1152)
-    gather[1].wait_recv()
-    acc[...] += slice_dot(head_at(-1), 0, 1152)
     gather[3].wait_recv()
-    acc[...] += slice_dot(head_at(1), 0, 1152)
-    gather[2].wait_recv()
+    acc[...] += slice_dot(left, 0, 1152)
+    gather[4].wait_recv()
+    acc[...] += slice_dot(right, 0, 1152)
+    for copy in (gather[2], forward[0], forward[1]):
+        copy.wait_recv()
     acc[:, 768:896] += slice_dot(head_at(2), 768, 896)
     acc[:, 0:256] = rounded(acc[:, 0:256] + slice_dot(head_at(2), 0, 256))
     acc[:, 256:768] = rounded(acc[:, 256:768] + slice_dot(head_at(2), 256, 768))
 
+    def short_conv(col, tap):
+        cols = slice(col, col + 128)
+        weights = conv[:, tap : tap + 128]
+        total = acc[HALO:, cols] * weights[3:4]
+        for n in range(3):
+            total += acc[HALO - 3 + n : HALO - 3 + n + rows, cols] * weights[n : n + 1] * taps[n]
+        return silu(total)
+
+    def unit(matrix):
+        return matrix * lax.rsqrt(jnp.sum(matrix * matrix, axis=-1, keepdims=True) + 1e-06)
+
+
+    k_unit = [unit(short_conv(128 * n, 128 * n)) for n in range(2)]
+    k_bf = [k.astype(bf16) for k in k_unit]
+    k_dots = [dot_t(k, k) for k in k_bf]
+    k_trans = [k.T for k in k_unit]
     ab = acc[HALO:, 768:896]
     pre = ab + dt_row
     gate = -rate_row * (jnp.maximum(pre, 0.0) + jnp.log1p(jnp.exp(-jnp.abs(pre))))
@@ -280,24 +308,9 @@
     cum_row = cum.T
     carried = jnp.exp(cum) * cmask[...]
 
-    def short_conv(col, tap):
-        cols = slice(col, col + 128)
-        weights = conv[:, tap : tap + 128]
-        total = acc[HALO:, cols] * weights[3:4]
-        for n in range(3):
-            total += acc[HALO - 3 + n : HALO - 3 + n + rows, cols] * weights[n : n + 1] * taps[n]
-        return silu(total)
-
-    def unit(matrix):
-        return matrix * lax.rsqrt(jnp.sum(matrix * matrix, axis=-1, keepdims=True) + 1e-06)
-
     def decay_of(h):
         return jnp.exp(cum[:, h : h + 1] - cum_row[h : h + 1, :] + neg[...])
 
-    k_unit = [unit(short_conv(128 * n, 128 * n)) for n in range(2)]
-    k_bf = [k.astype(bf16) for k in k_unit]
-    k_dots = [dot_t(k, k) for k in k_bf]
-    k_trans = [k.T for k in k_unit]
     last_rows = []
     for h in every:
         kh = h // 2
@@ -315,17 +328,17 @@
     row16, col16 = iotas(16, 256)
     eye16 = (row16 == (col16 & 15)).astype(f32)
     a8 = [abuf[h] * mm[0] for h in every]
-    a8c = [sum(a8[h][16 * n : 16 * n + 16, :].astype(f32) for n in range(16)) for h in every]
-    p2 = [dot(a8c[h].astype(bf16), a8[h]) for h in every]
+    a8c = [sum(a8[h][16 * n : 16 * n + 16, :] for n in range(1, 16)) + a8[h][0:16, :] for h in every]
+    p2 = [dot(a8c[h], a8[h]) for h in every]
     p2f = [expand(p2[h], 0) for h in every]
-    x1 = [eye16 - a8c[h] for h in every]
+    x1 = [eye16 - a8c[h].astype(f32) for h in every]
     x2 = [x1[h] + dot(x1[h].astype(bf16), p2f[h]) for h in every]
     p4 = [dot(p2[h].astype(bf16), p2f[h]) for h in every]
     p4f = [expand(p4[h], 0) for h in every]
     d = [x2[h] + dot(x2[h].astype(bf16), p4f[h]) for h in every]
     y = [dot(d[h].astype(bf16), abuf[h] * mm[1]) for h in every]
     d = [d[h] - dot(y[h].astype(bf16), expand(d[h], 0)) for h in every]
-    for n, size in enumerate((16, 32, 64, 128)):
+    for n, size in enumerate((16, 32, 64)):
         odd = (lax.broadcasted_iota(jnp.int32, (1, 256), 1) & size) != 0
         y = [dot(d[h].astype(bf16), abuf[h] * mm[n + 2]) for h in every]
         z = [dot(y[h].astype(bf16), expand(d[h], n)) for h in every]
@@ -333,8 +346,14 @@
             jnp.concatenate([jnp.where(odd, 0.0, d[h]), jnp.where(odd, d[h], 0.0) - z[h]], axis=0)
             for h in every
         ]
+    upper = [d[h][:, 0:128].astype(bf16) for h in every]
+    lower = [d[h][:, 128:256].astype(bf16) for h in every]
+    x_up = [dot(upper[h], kvb[h, 0:128, :]).astype(bf16) for h in every]
+    y = [dot(lower[h], abuf[h, 128:256, 0:128]).astype(bf16) for h in every]
+    x_low = [dot(lower[h], kvb[h, 128:256, :]) for h in every]
     for h in every:
-        wub[h] = dot(d[h].astype(bf16), kvb[h]).astype(bf16)
+        wub[h, 0:128, :] = x_up[h]
+        wub[h, 128:256, :] = (x_low[h] - dot(y[h], x_up[h])).astype(bf16)
 
     row_k, col_k = iotas(128, 128)
     for h in every:
@@ -413,9 +432,10 @@
     for copy in use_copy:
         copy.wait_recv()
 
-    chunk = rows // 2
+    chunks = 4
+    chunk = rows // chunks
     rs_copy = []
-    for c in range(2):
+    for c in range(chunks):
         span = slice(chunk * c, chunk * c + chunk)
         gated = []
         for h in every:
@@ -437,7 +457,7 @@
             copy.start()
             rs_copy.append(copy)
         osum[span, :] = dot(gated, wo[:, pl.ds(pl.multiple_of(j * feat, feat), feat)])
-    for c in range(2):
+    for c in range(chunks):
         span = slice(chunk * c, chunk * c + chunk)
         for copy in rs_copy[3 * c : 3 * c + 3]:
             copy.wait_recv()
@@ -446,7 +466,7 @@
             total += rbuf[n, span, :].astype(f32)
         out[span, :] = total.astype(bf16)
 
-    gathers = [gather[d] for d in (1, 3, 2)]
+    gathers = gather + forward
     for copy in gathers + to_copy + use_copy + rs_copy:
         copy.wait_send()
     for step, copies in ((1, halo), (2, next_copy), (4, after_copy)):
@@ -521,18 +541,18 @@
             dma((15,)),
             dma((4,)),
             dma((4,)),
-            dma((3,)),
-            dma((3,)),
-            dma((2,)),
-            dma((2,)),
-            dma((2,)),
-            dma((2,)),
-            dma((2,)),
-            dma((2,)),
-            dma((2,)),
-            dma((2,)),
-            dma((2, 3)),
-            dma((2, 3)),
+            dma((7,)),
+            dma((7,)),
+            dma((2,)),
+            dma((2,)),
+            dma((2,)),
+            dma((2,)),
+            dma((2,)),
+            dma((2,)),
+            dma((2,)),
+            dma((2,)),
+            dma((4, 3)),
+            dma((4, 3)),
         ],
         compiler_params=pltpu.CompilerParams(
             collective_id=0, has_side_effects=True, vmem_limit_bytes=60 * 1024 * 1024

time: 40.6 us -> 40.4 us (level)
  no operation moved by 1% of the time
where the time goes in v4:
time: 40.4 us; the launch traced here: 40.1 us
  Pallas kernels  38.5 us (95%)
  local copies, waits for them, and re-layouts  1.57 us (4%)
    pallas_call x1, Pallas kernels, body(): pl.pallas_call(lambda *refs: layer_kernel(n_ctx, n_head, *refs), out_shap...  38.5 us
    unnamed x1, local copies, waits for them, and re-layouts  1.57 us

profile of v4, /device:TPU:449, one launch (start us, length us, event | category | flops | bytes accessed | tf_op | source)
XLA Modules:
  0.0 40.1 jit_solution(5088526339363745634)
XLA Ops:
  0.0 38.5 %delta_layer.1 = bf16[256,256]{1,0:T(8,128)(2,1)} custom-call(s32[64]{0:T(128)} %refs_0_.1, f32[4]{0:T(128)} %refs_1_.1, f32[4]{0:T(128)} %refs_2_.1, bf16[256,256]{1,0:T(8,128)(2,1)} %refs_3_.1, bf16[1024,256]{1,0:T(8,128)(2,1)} %refs_4_.1, bf16[1024,256]{1,0:T(8,128)(2,1)} %refs_5_.1, bf16[1024,512]{1,0:T(8,128)(2,1)} %refs_6_.1, ...), custom_call_target="tpu_custom_call" | custom-call | tf_op jit(solution)/shard_map/delta_layer/pallas_call | solution.py:502
  38.5 1.6 %copy.17 = bf16[256,256]{1,0:T(8,128)(2,1)} copy(bf16[256,256]{1,0:T(8,128)(2,1)} %delta_layer.1) | data formatting | bytes 262144

commit v5 on v4

--- a/solution.py
+++ b/solution.py
@@ -98,6 +98,7 @@
     use_recv,
     rs_send,
     rs_recv,
+    ready,
 ):
     rows = tok.shape[0]
     feat = tok.shape[1]
@@ -119,18 +120,20 @@
     mate = (i + 1 - 2 * core, j)
 
     barrier = pltpu.get_barrier_semaphore()
-    def greet(*to):
-        for one in to:
-            pl.semaphore_signal(barrier, inc=1, device_id=one, device_id_type=MESH)
-
-    greet(*[(i, head_at(d)) for d in (1, 2, 3)])
-    pl.when(there(-1))(lambda: greet(*[(ctx_at(-1), head_at(d)) for d in every]))
-    pl.when(core == 0)(lambda: greet((ctx_at(1), j)))
-    pl.when(there(-2))(lambda: greet((ctx_at(-2), j)))
-    pl.when(there(-4))(lambda: greet((ctx_at(-4), j)))
-    expected = 3 + core + sum(
-        jnp.where(there(step), number, 0) for step, number in ((1, 4), (2, 1), (4, 1))
-    )
+    def tell(semaphore, to):
+        pl.semaphore_signal(semaphore, inc=1, device_id=to, device_id_type=MESH)
+
+    for d in (1, 2, 3):
+        tell(barrier, (i, head_at(d)))
+    pl.when(there(1))(lambda: tell(barrier, (ctx_at(1), j)))
+    pl.when(there(-1))(lambda: tell(barrier, (ctx_at(-1), j)))
+    expected = 3 + jnp.where(there(1), 1, 0) + jnp.where(there(-1), 1, 0)
+
+    def pass_on(level):
+        pl.when(there(level + 1) & there(-1))(lambda: tell(ready.at[level], (ctx_at(-1), j)))
+
+    def hear(level):
+        pl.when(there(level + 2))(lambda: pl.semaphore_wait(ready.at[level], 1))
 
     loads = [
         (tok, xg.at[j, pl.ds(HALO, rows), :]),
@@ -157,15 +160,23 @@
             src_ref=src, dst_ref=dst, send_sem=send, recv_sem=recv, device_id=to, device_id_type=MESH
         )
 
-    halo = [
+    first_rows = pl.ds(0, HALO)
+    halo = remote(
+        tok.at[pl.ds(rows - HALO, HALO), :],
+        xg.at[j, first_rows, :],
+        halo_send.at[0],
+        halo_recv.at[0],
+        (ctx_at(1), j),
+    )
+    halo_on = [
         remote(
-            tok.at[pl.ds(rows - HALO, HALO), :],
-            xg.at[j, pl.ds(0, HALO), :],
+            xg.at[j, first_rows, :],
+            xg.at[j, first_rows, :],
             halo_send.at[d],
             halo_recv.at[d],
-            (ctx_at(1), head_at(d)),
+            (i, head_at(d)),
         )
-        for d in every
+        for d in (2, 1, 3)
     ]
     edge = rows // 4
     right, left = head_at(1), head_at(-1)
@@ -186,14 +197,10 @@
     ]
     forward = [move(5, left, 0, edge, right), move(6, right, rows - edge, edge, left)]
     pl.semaphore_wait(barrier, expected)
+    pl.when(there(1))(halo.start)
     for copy in gather:
         copy.start()
-
-    @pl.when(there(1))
-    def _():
-        for copy in halo:
-            copy.start()
-
+    pass_on(0)
     for copy in loads:
         copy.start()
 
@@ -246,6 +253,19 @@
         gather[n].wait_recv()
         forward[n].start()
 
+    @pl.when(there(-1))
+    def _():
+        halo.wait_recv()
+        for copy in halo_on:
+            copy.start()
+
+    @pl.when(i == 0)
+    def _():
+        xg[:, 0:HALO, :] = jnp.zeros((4, HALO, feat), bf16)
+
+    hear(0)
+    pass_on(1)
+
     for copy in loads[:9]:
         copy.wait()
     wab_t = jnp.concatenate(
@@ -260,16 +280,14 @@
     def rounded(value):
         return value.astype(bf16).astype(f32)
 
+    acc[...] = slice_dot(j, 0, 1152)
+    hear(1)
+    pass_on(2)
     @pl.when(there(-1))
     def _():
-        for copy in halo:
+        for copy in halo_on:
             copy.wait_recv()
 
-    @pl.when(i == 0)
-    def _():
-        xg[:, 0:HALO, :] = jnp.zeros((4, HALO, feat), bf16)
-
-    acc[...] = slice_dot(j, 0, 1152)
     gather[3].wait_recv()
     acc[...] += slice_dot(left, 0, 1152)
     gather[4].wait_recv()
@@ -363,6 +381,7 @@
         to_s[h, :, 0:128] = (passed - step[:, 0:128]).astype(bf16)
         to_s[h, :, 128:256] = step[:, 128:256].astype(bf16)
 
+    hear(2)
     to_copy = [
         remote(to_s.at[2 - 2 * core + n], pair.at[core, n], to_send.at[n], to_recv.at[n], mate)
         for n in range(2)
@@ -469,7 +488,7 @@
     gathers = gather + forward
     for copy in gathers + to_copy + use_copy + rs_copy:
         copy.wait_send()
-    for step, copies in ((1, halo), (2, next_copy), (4, after_copy)):
+    for step, copies in ((1, [halo]), (-1, halo_on), (2, next_copy), (4, after_copy)):
 
         @pl.when(there(step))
         def _(copies=copies):
@@ -553,6 +572,7 @@
             dma((2,)),
             dma((4, 3)),
             dma((4, 3)),
+            pltpu.SemaphoreType.REGULAR((3,)),
         ],
         compiler_params=pltpu.CompilerParams(
             collective_id=0, has_side_effects=True, vmem_limit_bytes=60 * 1024 * 1024

time: 40.4 us -> 39.9 us (0.988)
  Pallas kernels: 38.5 us -> 37.8 us
    pallas_call x1, Pallas kernels: 38.5 us -> 37.8 us  [body(): pl.pallas_call(lambda *refs: layer_kernel(n_ctx, n_head, *refs), out_shap...]
where the time goes in v5:
time: 39.9 us; the launch traced here: 39.4 us
  Pallas kernels  37.8 us (95%)
  local copies, waits for them, and re-layouts  1.57 us (4%)
    pallas_call x1, Pallas kernels, body(): pl.pallas_call(lambda *refs: layer_kernel(n_ctx, n_head, *refs), out_shap...  37.8 us
    unnamed x1, local copies, waits for them, and re-layouts  1.57 us

profile of v5, /device:TPU:449, one launch (start us, length us, event | category | flops | bytes accessed | tf_op | source)
XLA Modules:
  0.0 39.4 jit_solution(16635439909073494750)
XLA Ops:
  0.0 37.8 %delta_layer.1 = bf16[256,256]{1,0:T(8,128)(2,1)} custom-call(s32[64]{0:T(128)} %refs_0_.1, f32[4]{0:T(128)} %refs_1_.1, f32[4]{0:T(128)} %refs_2_.1, bf16[256,256]{1,0:T(8,128)(2,1)} %refs_3_.1, bf16[1024,256]{1,0:T(8,128)(2,1)} %refs_4_.1, bf16[1024,256]{1,0:T(8,128)(2,1)} %refs_5_.1, bf16[1024,512]{1,0:T(8,128)(2,1)} %refs_6_.1, ...), custom_call_target="tpu_custom_call" | custom-call | tf_op jit(solution)/shard_map/delta_layer/pallas_call | solution.py:521
  37.8 1.6 %copy.17 = bf16[256,256]{1,0:T(8,128)(2,1)} copy(bf16[256,256]{1,0:T(8,128)(2,1)} %delta_layer.1) | data formatting | bytes 262144

commit v6 on v5

--- a/solution.py
+++ b/solution.py
@@ -520,7 +520,7 @@
     dma = pltpu.SemaphoreType.DMA
     return pl.pallas_call(
         lambda *refs: layer_kernel(n_ctx, n_head, *refs),
-        out_shape=jax.ShapeDtypeStruct((rows, feat), bf16),
+        out_shape=pltpu.VMEM((rows, feat), bf16),
         in_specs=[hbm] * 15,
         out_specs=pl.BlockSpec(memory_space=pltpu.VMEM),
         scratch_shapes=[

time: 39.9 us -> 38.3 us (0.960)
  local copies, waits for them, and re-layouts: 1.57 us -> 0.66 us
  Pallas kernels: 37.8 us -> 37.2 us
    unnamed x1, local copies, waits for them, and re-layouts: 1.57 us -> 0.66 us
    pallas_call x1, Pallas kernels: 37.8 us -> 37.2 us  [body(): pl.pallas_call(lambda *refs: layer_kernel(n_ctx, n_head, *refs), out_shap...]
where the time goes in v6:
time: 38.3 us; the launch traced here: 37.9 us
  Pallas kernels  37.2 us (97%)
  local copies, waits for them, and re-layouts  0.66 us (2%)
    pallas_call x1, Pallas kernels, body(): pl.pallas_call(lambda *refs: layer_kernel(n_ctx, n_head, *refs), out_shap...  37.2 us

profile of v6, /device:TPU:449, one launch (start us, length us, event | category | flops | bytes accessed | tf_op | source)
XLA Modules:
  0.0 37.9 jit_solution(13516250164747401454)
XLA Ops:
  0.0 37.2 %delta_layer.1 = bf16[256,256]{1,0:T(8,128)(2,1)S(1)} custom-call(s32[64]{0:T(128)} %refs_0_.1, f32[4]{0:T(128)} %refs_1_.1, f32[4]{0:T(128)} %refs_2_.1, bf16[256,256]{1,0:T(8,128)(2,1)} %refs_3_.1, bf16[1024,256]{1,0:T(8,128)(2,1)} %refs_4_.1, bf16[1024,256]{1,0:T(8,128)(2,1)} %refs_5_.1, bf16[1024,512]{1,0:T(8,128)(2,1)} %refs_6_.1, ...), custom_call_target="tpu_custom_call" | custom-call | tf_op jit(solution)/shard_map/delta_layer/pallas_call | solution.py:521
  37.2 0.7 %copy.17 = bf16[256,256]{1,0:T(8,128)(2,1)} copy(bf16[256,256]{1,0:T(8,128)(2,1)S(1)} %delta_layer.1) | data formatting | bytes 262144
